TPU v7x, 32 devices: a whole 2x2x4 slice. The times are simulated.
32 devices in a mesh: vocab: 8 (over z, x), dp: 4 (over y, core).
Axes of the slice: x: 2, y: 2, z: 4, core: 2. Of those that a mesh axis runs over, the one named last changes fastest.
Arguments:
- hidden: bfloat16 [1024, 8192], P('dp', 'vocab'), may hold values from -49.67767 to 49.67767
- targets: int32 [1024], P('dp'), may hold values from 0 to 2047
- loss_mask: int32 [1024], P('dp'), may hold values from 0 to 1, as said below
- master: float32 [2048, 8192], P(('vocab', 'dp')), may hold values from -1 to 1
- first_moment: float32 [2048, 8192], P(('vocab', 'dp')), may hold values from -0.00390625 to 0.00390625
- second_moment: float32 [2048, 8192], P(('vocab', 'dp')), may hold values from 1.4901161e-08 to 2.3841858e-07
Outputs:
- loss_value: float32 [], replicated
- hidden_grad: bfloat16 [1024, 8192], P('dp', 'vocab')
- new_master: float32 [2048, 8192], P(('vocab', 'dp'))
- new_first: float32 [2048, 8192], P(('vocab', 'dp'))
- new_second: float32 [2048, 8192], P(('vocab', 'dp'))
Inputs may be any that keep to these rules, and one draw needn't show every extreme that they name: `loss_mask`: the first position of every aligned block of 256 positions is 1.
All inputs are finite; a program needn't handle non-finite values.
Results may differ from a plain program's by a relative error of at most 0.02.
Values may be sent and summed in bfloat16 or wider, within the bound.
A program may use at most 128 MiB of HBM per device.

v0:
```python
import jax
import jax.numpy as jnp
from jax import lax
from jax.sharding import PartitionSpec as P

STEP = 10


beta_one = 0.9
beta_two = 0.95
learn_rate = 0.0003
decay_rate = 0.1
epsilon_adam = 1e-08
clip_norm = 1.0


def on_device(hidden, targets, loss_mask, master, first_moment, second_moment):
    weights_half = master.astype(jnp.bfloat16)
    gathered = lax.all_gather(hidden, "vocab", axis=1, tiled=True)
    shard_rows = weights_half.shape[0]
    local_vocab = shard_rows * lax.axis_size("dp")
    full_head = lax.all_gather(weights_half, "dp", axis=0, tiled=True)
    logits = jnp.einsum("td,vd->tv", gathered, full_head, preferred_element_type=jnp.float32)
    offset = lax.axis_index("vocab") * local_vocab
    local_ids = targets - offset
    columns = lax.broadcasted_iota(jnp.int32, (1, local_vocab), 1)
    onehot = (columns == local_ids[:, None]).astype(jnp.float32)
    picked_local = jnp.sum(onehot * logits, axis=1)
    row_top = lax.pmax(jnp.max(logits, axis=1), "vocab")
    sum_local = jnp.sum(jnp.exp(logits - row_top[:, None]), axis=1)
    exp_sum, picked = lax.psum((sum_local, picked_local), "vocab")
    log_norm = row_top + jnp.log(exp_sum)
    mask_float = loss_mask.astype(jnp.float32)
    token_loss = mask_float * (log_norm - picked)
    logit_grad = (mask_float[:, None] * (jnp.exp(logits - log_norm[:, None]) - onehot)).astype(
        jnp.bfloat16
    )
    hidden_term = (
        lax.psum_scatter(
            jnp.einsum(
                "tv,vc->ct", logit_grad, full_head, preferred_element_type=jnp.float32
            ).astype(jnp.bfloat16),
            "vocab",
            scatter_dimension=0,
            tiled=True,
        )
        .astype(jnp.float32)
        .T
    )
    weight_raw = lax.psum_scatter(
        jnp.einsum("tv,td->vd", logit_grad, gathered, preferred_element_type=jnp.float32).astype(
            jnp.bfloat16
        ),
        "dp",
        scatter_dimension=0,
        tiled=True,
    ).astype(jnp.float32)
    count_local = jnp.sum(mask_float)
    loss_local = jnp.sum(token_loss)
    valid_count, loss_sum = lax.psum((count_local, loss_local), "dp")
    weight_grad = weight_raw / valid_count
    square_sum = lax.psum(jnp.sum(weight_grad * weight_grad), ("vocab", "dp"))
    grad_norm = jnp.sqrt(square_sum)
    hidden_grad = (hidden_term / valid_count).astype(jnp.bfloat16)
    loss_value = loss_sum / valid_count
    clip_factor = jnp.minimum(1.0, clip_norm / (grad_norm + 1e-06))
    clipped = weight_grad * clip_factor
    new_first = beta_one * first_moment + (1.0 - beta_one) * clipped
    new_second = beta_two * second_moment + (1.0 - beta_two) * clipped * clipped
    first_bias = 1.0 - beta_one**STEP
    second_bias = 1.0 - beta_two**STEP
    update = (
        new_first / first_bias / (jnp.sqrt(new_second / second_bias) + epsilon_adam)
        + decay_rate * master
    )
    new_master = master - learn_rate * update
    return (loss_value, hidden_grad, new_master, new_first, new_second)


def solution(mesh):
    placed = (
        P("dp", "vocab"),
        P("dp"),
        P("dp"),
        P(("vocab", "dp"), None),
        P(("vocab", "dp"), None),
        P(("vocab", "dp"), None),
    )
    return jax.shard_map(
        on_device,
        mesh=mesh,
        in_specs=placed,
        out_specs=(
            P(),
            P("dp", "vocab"),
            P(("vocab", "dp"), None),
            P(("vocab", "dp"), None),
            P(("vocab", "dp"), None),
        ),
        check_vma=False,
    )
```

profile of v0, /device:TPU:0, one launch (start us, length us, event | category | flops | bytes accessed | tf_op | source)
XLA Modules:
  0.0 323.3 jit_solution(14633085906508373005)
XLA Ops:
  7.2 0.0 copy-start.1
  7.2 0.0 copy-start.2
  7.2 0.0 all-gather.5.cloned.1.call-start
  7.2 2.7 convert_element_type.34
  9.9 0.0 all-gather.5.cloned.1.call-update
  9.9 0.0 all-gather.3.cloned.1.call-start
  10.0 0.7 all-gather.3.cloned.1.call-update
  10.7 0.0 reduce-scatter.5.cloned.1.call-start
  10.7 0.0 copy-done.1
  10.8 0.0 copy-done.2
  10.8 36.6 %all-gather.5.cloned.1.call-done = bf16[256,8192]{1,0:T(8,128)(2,1)} async-done(((bf16[64,8192]{1,0:T(8,128)(2,1)}), bf16[256,8192]{1,0:T(8,128)(2,1)}) %all-gather.5.cloned.1.call-update) | async-done | bytes 4194320 | tf_op jit(solution)/shard_map/all_gather | solution.py:22
  47.4 75.6 %all-gather.3.cloned.1.call-done = bf16[256,8192]{1,0:T(8,128)(2,1)} async-done(((bf16[256,1024]{1,0:T(8,128)(2,1)}), bf16[256,8192]{1,0:T(8,128)(2,1)}) %all-gather.3.cloned.1.call-update) | async-done | bytes 4194320 | tf_op jit(solution)/shard_map/all_gather | solution.py:19
  123.0 4.8 %fusion.4 = (f32[256]{0:T(256)S(1)}, f32[256,256]{0,1:T(8,128)S(1)}) fusion(bf16[256,8192]{1,0:T(8,128)(2,1)} %all-gather.3.cloned.1.call-done, bf16[256,8192]{1,0:T(8,128)(2,1)} %all-gather.5.cloned.1.call-done), kind=kOutput, calls=%fused_computation.19 | convolution fusion | flops 1073807104 | bytes 8651776 | tf_op jit(solution)/shard_map/td,vd->tv/dot_general | solution.py:23
  127.7 18.7 %pmax.7 = f32[256]{0:T(256)S(1)} all-reduce(f32[256]{0:T(256)S(1)} %get-tuple-element.17), channel_id=1, replica_groups=mesh['vocab'=8,'dp'=4] {'vocab'}, use_global_device_ids=true, to_apply=%region_1.0 | all-reduce | flops 256 | bytes 2048 | tf_op jit(solution)/shard_map/pmax | solution.py:29
  146.4 0.1 select_reduce_fusion
  146.5 17.5 %all-reduce = (f32[256]{0:T(256)S(1)}, f32[256]{0:T(256)S(1)}) all-reduce(f32[256]{0:T(256)S(1)} %get-tuple-element.6, f32[256]{0:T(256)S(1)} %get-tuple-element.5), channel_id=1, replica_groups=mesh['vocab'=8,'dp'=4] {'vocab'}, use_global_device_ids=true, to_apply=%region_3.0 | all-reduce | flops 512 | bytes 4096 | tf_op jit(solution)/shard_map/psum | solution.py:31
  164.1 0.6 convert_reduce_fusion
  164.7 5.4 %convolution_convert_fusion = bf16[256,8192]{1,0:T(8,128)(2,1)} fusion(bf16[256,8192]{1,0:T(8,128)(2,1)} %all-gather.3.cloned.1.call-done, f32[256,256]{0,1:T(8,128)S(1)} %get-tuple-element.18, f32[256]{0:T(256)S(1)} %get-tuple-element.16, f32[256]{0:T(256)S(1)} %convert_element_type.33, s32[256]{0:T(256)S(1)} %broadcast_subtract_fusion), kind=kOutput, calls=%fused_computation | convolution fusion | flops 1076232192 | bytes 8653824 | tf_op jit(solution)/shard_map/tv,td->vd/dot_general | solution.py:51
  170.1 0.0 reduce-scatter.5.cloned.1.call-update
  170.1 0.0 reduce-scatter.3.cloned.1.call-start
  170.2 5.5 %fusion = bf16[8192,256]{0,1:T(8,128)(2,1)} fusion(bf16[256,8192]{1,0:T(8,128)(2,1)} %all-gather.5.cloned.1.call-done, f32[256,256]{0,1:T(8,128)S(1)} %get-tuple-element.18, f32[256]{0:T(256)S(1)} %get-tuple-element.16, f32[256]{0:T(256)S(1)} %convert_element_type.33, s32[256]{0:T(256)S(1)} %broadcast_subtract_fusion), kind=kOutput, calls=%fused_computation.2 | convolution fusion | flops 1076232192 | bytes 8653824 | tf_op jit(solution)/shard_map/tv,vc->ct/dot_general | solution.py:40
  175.6 0.0 reduce-scatter.3.cloned.1.call-update
  175.7 0.0 copy-start
  175.7 6.4 %all-reduce.1 = (f32[]{:T(128)}, f32[]{:T(128)}) all-reduce(f32[]{:T(128)} %get-tuple-element.8, f32[]{:T(128)} %get-tuple-element.7), channel_id=1, replica_groups=mesh['vocab'=8,'dp'=4] {'dp'}, use_global_device_ids=true, to_apply=%region_7.0 | all-reduce | flops 2 | bytes 16 | tf_op jit(solution)/shard_map/psum | solution.py:60
  182.1 30.9 %reduce-scatter.5.cloned.1.call-done = bf16[64,8192]{1,0:T(8,128)(2,1)} async-done(((bf16[256,8192]{1,0:T(8,128)(2,1)}), bf16[64,8192]{1,0:T(8,128)(2,1)}) %reduce-scatter.5.cloned.1.call-update) | async-done | bytes 1048592 | tf_op jit(solution)/shard_map/reduce_scatter | solution.py:50
  213.0 2.9 multiply_reduce_fusion
  217.2 41.8 %psum.39 = f32[]{:T(128)} all-reduce(f32[]{:T(128)} %multiply_reduce_fusion), channel_id=1, replica_groups=mesh['vocab'=8,'dp'=4] {'vocab','dp'}, use_global_device_ids=true, to_apply=%region_13.0 | all-reduce | flops 1 | bytes 8 | tf_op jit(solution)/shard_map/psum | solution.py:62
  259.7 46.6 %reduce-scatter.3.cloned.1.call-done = bf16[1024,256]{0,1:T(8,128)(2,1)} async-done(((bf16[8192,256]{0,1:T(8,128)(2,1)}), bf16[1024,256]{0,1:T(8,128)(2,1)}) %reduce-scatter.3.cloned.1.call-update) | async-done | bytes 524304 | tf_op jit(solution)/shard_map/reduce_scatter | solution.py:39
  306.3 2.5 fusion.2
  308.8 0.0 copy-done
  308.8 6.9 %multiply_subtract_fusion = (f32[64,8192]{1,0:T(8,128)}, f32[64,8192]{1,0:T(8,128)}, f32[64,8192]{1,0:T(8,128)}) fusion(f32[64,8192]{1,0:T(8,128)S(1)} %copy-done, f32[]{:T(128)S(6)} %min.3, f32[]{:T(128)} %get-tuple-element.12, bf16[64,8192]{1,0:T(8,128)(2,1)} %reduce-scatter.5.cloned.1.call-done, f32[64,8192]{1,0:T(8,128)} %param.10, f32[64,8192]{1,0:T(8,128)} %param.11), kind=kLoop, calls=%fused_computation.5 | loop fusion | flops 9437184 | bytes 13631496 | tf_op jit(solution)/shard_map/sub | solution.py:76
  (2 shorter events, 0.0 us)
Async XLA Ops:
  7.2 3.6 %copy-start.1 = (s32[256]{0:T(256)S(1)}, s32[256]{0:T(256)}, u32[]{:S(2)}) copy-start(s32[256]{0:T(256)} %param.8) | copy-start | bytes 3076
  7.2 3.6 %copy-start.2 = (s32[256]{0:T(256)S(1)}, s32[256]{0:T(256)}, u32[]{:S(2)}) copy-start(s32[256]{0:T(256)} %param.7) | copy-start | bytes 3076
  7.2 40.2 %all-gather.5.cloned.1.call-start = ((), (), s32[]{:S(2)}) async-start(), calls=%async_computation.3 | async-start | bytes 5242880 | tf_op jit(solution)/shard_map/all_gather | solution.py:22
  9.9 113.0 %all-gather.3.cloned.1.call-start = ((), (), s32[]{:S(2)}) async-start(), calls=%async_computation.2 | async-start | bytes 4718592 | tf_op jit(solution)/shard_map/all_gather | solution.py:19
  10.7 202.4 %reduce-scatter.5.cloned.1.call-start = ((), (), s32[]{:S(2)}) async-start(), calls=%async_computation.5 | async-start | bytes 5242880 | tf_op jit(solution)/shard_map/reduce_scatter | solution.py:50
  170.1 136.2 %reduce-scatter.3.cloned.1.call-start = ((), (), s32[]{:S(2)}) async-start(), calls=%async_computation.4 | async-start | bytes 4718592 | tf_op jit(solution)/shard_map/reduce_scatter | solution.py:39
  175.7 133.1 %copy-start = (f32[64,8192]{1,0:T(8,128)S(1)}, f32[64,8192]{1,0:T(8,128)}, u32[]{:S(2)}) copy-start(f32[64,8192]{1,0:T(8,128)} %param.9) | copy-start | bytes 6291460
Sparse Core Ops, SparseCore 0:
  10.2 37.1 all-gather.4
  49.6 73.3 all-gather.2
  170.2 42.7 reduce-scatter.4
  216.9 89.2 reduce-scatter.2
where the time goes:
time: 324 us; the launch traced here: 323 us
  waiting for transfers between devices  190 us (59%)
  blocking collectives  84.5 us (26%)
  between operations  16.9 us (5%)
  other arithmetic  15.6 us (5%)
  matrix products  15.6 us (5%)
    all_gather x1, waiting for transfers between devices, on_device(): gathered = lax.all_gather(hidden, 'vocab', axis=1, tiled=True)  75.6 us
    reduce_scatter x1, waiting for transfers between devices, on_device(): lax.psum_scatter(jnp.einsum('tv,vc->ct', logit_grad, full_head, preferred...  46.6 us
    psum x1, blocking collectives, on_device(): square_sum = lax.psum(jnp.sum(weight_grad * weight_grad), ('vocab', 'dp'))  41.8 us
    all_gather x1, waiting for transfers between devices, on_device(): full_head = lax.all_gather(weights_half, 'dp', axis=0, tiled=True)  36.6 us
    reduce_scatter x1, waiting for transfers between devices, on_device(): lax.psum_scatter(jnp.einsum('tv,td->vd', logit_grad, gathered, preferred_...  30.9 us
    pmax x1, blocking collectives, on_device(): row_top = lax.pmax(jnp.max(logits, axis=1), 'vocab')  18.7 us
    psum x1, blocking collectives, on_device(): exp_sum, picked = lax.psum((sum_local, picked_local), 'vocab')  17.5 us
    sub x1, other arithmetic, on_device(): new_master = master - learn_rate * update  6.86 us
  transfers between devices with their start and end apart: 4, of which 4 were waited for; matrix products, arithmetic and copies ran while one was open for 3% of the time, Pallas kernels for 0%

commit v1 on v0

v1 whole, which is shorter than its diff:
```python
import functools

import jax
import jax.numpy as jnp
from jax import lax
from jax.experimental import pallas as pl
from jax.experimental.pallas import tpu as pltpu
from jax.sharding import PartitionSpec as P

STEP = 10

beta_one = 0.9
beta_two = 0.95
learn_rate = 0.0003
decay_rate = 0.1
epsilon_adam = 1e-08
clip_norm = 1.0

MESH = pl.DeviceIdType.MESH
F32 = jnp.float32
BF16 = jnp.bfloat16


def kernel(
    n_vocab, n_dp,
    hid, master, targets, mask,
    hgrad_out, wgrad_out, scal_out,
    Wg, wsend, Hg, acc, lrecv, gt, gtp,
    htsend, htrecv, gsend, grecv, gown, ysend, yrecv, xsend, xrecv,
    stat, cnt, sqa, sqb,
    z_send, z_recv, wx_send, wy_send, ws_send, w_recv,
    l_send, l_recv, st_send, st_recv, ht_send, ht_recv,
    g_send, g_recv, y_send, y_recv, x_send, x_recv,
    c_send, c_recv, a_send, a_recv, b_send, b_recv,
):
    n_o = n_vocab // 2
    n_y = n_dp // 2
    v = lax.axis_index("vocab")
    r = lax.axis_index("dp")
    o = v // 2
    i = v % 2
    y = r // 2
    c = r % 2
    rows = master.shape[0]
    blk = hid.shape[1]
    toks = hid.shape[0]
    group = 2 * n_dp * rows
    x_peer = (o * 2 + 1 - i, r)
    sibling = (v, y * 2 + 1 - c)

    def y_at(dy):
        return lax.rem(y + dy, n_y)

    def y_peer(dy):
        return (v, y_at(dy) * 2 + c)

    def rcopy(src, dst, ssem, rsem, dev):
        return pltpu.make_async_remote_copy(
            src_ref=src, dst_ref=dst, send_sem=ssem, recv_sem=rsem,
            device_id=dev, device_id_type=MESH,
        )

    barrier = pltpu.get_barrier_semaphore()
    for k in range(1, n_vocab):
        pl.semaphore_signal(barrier, inc=1, device_id=(lax.rem(v + k, n_vocab), r), device_id_type=MESH)
    for k in range(1, n_dp):
        pl.semaphore_signal(barrier, inc=1, device_id=(v, lax.rem(r + k, n_dp)), device_id_type=MESH)
    pl.semaphore_wait(barrier, n_vocab - 1 + n_dp - 1)

    sends = []

    def z_copy(src, b, side):
        peer = o + 1 if side == 0 else o - 1
        return rcopy(src, Hg.at[b], z_send.at[side, b], z_recv.at[b], (peer * 2 + i, r))

    @pl.when(o < n_o - 1)
    def _():
        z_copy(hid, o, 0).start()

    @pl.when(o > 0)
    def _():
        z_copy(hid, o, 1).start()

    def z_step(d, then):
        @pl.when(o - d >= 0)
        def _():
            b = o - d
            z_copy(hid, b, 0).wait_recv()

            @pl.when(o < n_o - 1)
            def _():
                z_copy(Hg.at[b], b, 0).start()

            then(b)

        @pl.when(o + d < n_o)
        def _():
            b = o + d
            z_copy(hid, b, 1).wait_recv()

            @pl.when(o > 0)
            def _():
                z_copy(Hg.at[b], b, 1).start()

            then(b)

    def slot(ii, rr):
        return pl.ds(pl.multiple_of((ii * n_dp + rr) * rows, rows), rows)

    def w_slot(ii, rr):
        return Wg.at[:, slot(ii, rr), :]

    def w_sem(ii, rr):
        return w_recv.at[ii * n_dp + rr]

    def w_y(dy, k, ii):
        return rcopy(w_slot(ii, r), w_slot(ii, r), wy_send.at[dy - 1, k], w_sem(ii, r), y_peer(dy))

    def w_s(dy, k, ii):
        rr = y_at(dy) * 2 + c
        return rcopy(w_slot(ii, rr), w_slot(ii, rr), ws_send.at[dy, k], w_sem(ii, rr), sibling)

    def w_wait(ii, rr):
        rcopy(w_slot(ii, rr), w_slot(ii, rr), wx_send.at[0], w_sem(ii, rr), x_peer).wait_recv()

    for b in range(n_o):
        cols = pl.ds(pl.multiple_of((2 * b + 1 - i) * blk, blk), blk)
        wsend[b] = master[:, cols].astype(BF16)
    wx = rcopy(wsend, w_slot(i, r), wx_send.at[0], w_sem(i, r), x_peer)
    wx.start()
    sends.append(wx)
    for b in range(n_o):
        cols = pl.ds(pl.multiple_of((2 * b + i) * blk, blk), blk)
        Wg[b, slot(i, r), :] = master[:, cols].astype(BF16)
    for dy in range(1, n_y):
        q = w_y(dy, 0, i)
        q.start()
        sends.append(q)
    q = w_s(0, 0, i)
    q.start()
    sends.append(q)

    maskf = mask[...].astype(F32)
    cnt[r] = jnp.broadcast_to(jnp.sum(maskf, axis=1, keepdims=True), cnt.shape[1:])
    for k in range(1, n_dp):
        q = rcopy(cnt.at[r], cnt.at[r], c_send.at[k], c_recv.at[r], (v, lax.rem(r + k, n_dp)))
        q.start()
        sends.append(q)
    Hg[o] = hid[...]
    acc[...] = jnp.zeros_like(acc)

    def nothing(b):
        return None

    w_wait(1 - i, r)
    for dy in range(1, n_y):
        q = w_y(dy, 1, 1 - i)
        q.start()
        sends.append(q)
    q = w_s(0, 1, 1 - i)
    q.start()
    sends.append(q)
    z_step(1, nothing)
    for dy in range(1, n_y):
        w_wait(i, y_at(dy) * 2 + c)
        q = w_s(dy, 0, i)
        q.start()
        sends.append(q)
    if n_o > 2:
        z_step(2, nothing)
    for dy in range(1, n_y):
        w_wait(1 - i, y_at(dy) * 2 + c)
        q = w_s(dy, 1, 1 - i)
        q.start()
        sends.append(q)
    for dy in range(n_y):
        for ii in range(2):
            w_wait(ii, y_at(dy) * 2 + 1 - c)

    def logits_of(b):
        acc[...] += lax.dot_general(
            Wg[b], Hg[b], (((1,), (1,)), ((), ())), preferred_element_type=F32
        )

    logits_of(o)
    for d in range(1, min(n_o, 3)):
        @pl.when(o - d >= 0)
        def _():
            logits_of(o - d)

        @pl.when(o + d < n_o)
        def _():
            logits_of(o + d)
    for d in range(3, n_o):
        z_step(d, logits_of)

    q = rcopy(acc, lrecv, l_send.at[0], l_recv.at[0], x_peer)
    q.start()
    q.wait()
    acc[...] = acc[...] + lrecv[...]

    logits = acc[...]
    ids = targets[...] - o * group
    onehot = (lax.broadcasted_iota(jnp.int32, (group, toks), 0) == ids).astype(F32)
    top = jnp.max(logits, axis=0, keepdims=True)
    stat[o] = jnp.zeros(stat.shape[1:], F32)
    stat[o, 0:1, :] = top
    stat[o, 1:2, :] = jnp.sum(jnp.exp(logits - top), axis=0, keepdims=True)
    stat[o, 2:3, :] = jnp.sum(onehot * logits, axis=0, keepdims=True)
    st = []
    for k in range(1, n_o):
        q = rcopy(stat.at[o], stat.at[o], st_send.at[k], st_recv.at[o], (lax.rem(o + k, n_o) * 2 + i, r))
        q.start()
        sends.append(q)
    for k in range(1, n_o):
        b = lax.rem(o + k, n_o)
        rcopy(stat.at[b], stat.at[b], st_send.at[k], st_recv.at[b], x_peer).wait_recv()
    row_top = stat[0, 0:1, :]
    for b in range(1, n_o):
        row_top = jnp.maximum(row_top, stat[b, 0:1, :])
    exp_sum = jnp.zeros_like(row_top)
    picked = jnp.zeros_like(row_top)
    for b in range(n_o):
        exp_sum += stat[b, 1:2, :] * jnp.exp(stat[b, 0:1, :] - row_top)
        picked += stat[b, 2:3, :]
    log_norm = row_top + jnp.log(exp_sum)
    loss_local = jnp.sum(maskf * (log_norm - picked), axis=1, keepdims=True)
    grad = maskf * (jnp.exp(acc[...] - log_norm) - onehot)
    gt[...] = grad.astype(BF16)

    g_tv = grad.T.astype(BF16)
    half = n_o // 2
    order = []
    for k in range(1, n_o):
        order.append(half + (k // 2) * (1 if k % 2 else -1))
    order = [k for k in order if 0 < k < n_o]
    for k in range(1, n_o):
        if k not in order:
            order.append(k)
    for k in order:
        b = lax.rem(o + k, n_o)
        htsend[k - 1] = jnp.dot(g_tv, Wg[b], preferred_element_type=F32).astype(BF16)
        q = rcopy(htsend.at[k - 1], htrecv.at[k - 1], ht_send.at[k - 1], ht_recv.at[k - 1], (b * 2 + i, r))
        q.start()
        sends.append(q)

    m = 0
    for cc in (1 - c, c):
        for dy in list(range(1, n_y)) + [0]:
            for ii in (1 - i, i):
                gtp[m * rows:(m + 1) * rows, :] = gt[slot(ii, y_at(dy) * 2 + cc), :]
                m += 1
    mid = group // 2
    for b in range(n_o):
        gsend[b] = jnp.dot(gtp[:mid, :], Hg[b], preferred_element_type=F32).astype(BF16)
        q = rcopy(gsend.at[b], grecv.at[b], g_send.at[b], g_recv.at[b], sibling)
        q.start()
        sends.append(q)
    for b in range(n_o):
        gown[b] = jnp.dot(gtp[mid:, :], Hg[b], preferred_element_type=F32)
    for b in range(n_o):
        rcopy(gsend.at[b], grecv.at[b], g_send.at[b], g_recv.at[b], sibling).wait_recv()
        for dy in range(1, n_y):
            part = slice((dy - 1) * 2 * rows, dy * 2 * rows)
            ysend[dy - 1, b] = (gown[b, part, :] + grecv[b, part, :].astype(F32)).astype(BF16)
            q = rcopy(
                ysend.at[dy - 1, b], yrecv.at[dy - 1, b], y_send.at[dy - 1, b], y_recv.at[dy - 1, b], y_peer(dy)
            )
            q.start()
            sends.append(q)
    htown = jnp.dot(g_tv, Wg[o], preferred_element_type=F32)
    last = slice((n_y - 1) * 2 * rows, n_y * 2 * rows)
    squares = jnp.zeros((8, blk), F32)
    for b in range(n_o):
        total = gown[b, last, :] + grecv[b, last, :].astype(F32)
        for dy in range(1, n_y):
            rcopy(
                ysend.at[dy - 1, b], yrecv.at[dy - 1, b], y_send.at[dy - 1, b], y_recv.at[dy - 1, b], y_peer(dy)
            ).wait_recv()
            total += yrecv[dy - 1, b].astype(F32)
        xsend[b] = total[:rows].astype(BF16)
        q = rcopy(xsend.at[b], xrecv.at[b], x_send.at[b], x_recv.at[b], x_peer)
        q.start()
        sends.append(q)
        mine = total[rows:]
        wgrad_out[:, pl.ds(pl.multiple_of((2 * b + i) * blk, blk), blk)] = mine
        squares += jnp.sum((mine * mine).reshape(rows // 8, 8, blk), axis=0)
    for b in range(n_o):
        rcopy(xsend.at[b], xrecv.at[b], x_send.at[b], x_recv.at[b], x_peer).wait_recv()
        theirs = xrecv[b].astype(F32)
        wgrad_out[:, pl.ds(pl.multiple_of((2 * b + 1 - i) * blk, blk), blk)] = theirs
        squares += jnp.sum((theirs * theirs).reshape(rows // 8, 8, blk), axis=0)
    square = jnp.sum(jnp.sum(squares, axis=0, keepdims=True), axis=1, keepdims=True)

    sqa[r, 0:8, :] = jnp.broadcast_to(square, (8, 128))
    sqa[r, 8:16, :] = jnp.broadcast_to(loss_local, (8, 128))
    for k in range(1, n_dp):
        q = rcopy(sqa.at[r], sqa.at[r], a_send.at[k], a_recv.at[r], (v, lax.rem(r + k, n_dp)))
        q.start()
        sends.append(q)
    for k in range(1, n_dp):
        b = lax.rem(r + k, n_dp)
        rcopy(sqa.at[b], sqa.at[b], a_send.at[k], a_recv.at[b], x_peer).wait_recv()
        rcopy(cnt.at[b], cnt.at[b], c_send.at[k], c_recv.at[b], x_peer).wait_recv()
    both = sqa[0]
    count = cnt[0]
    for b in range(1, n_dp):
        both = both + sqa[b]
        count = count + cnt[b]
    sqb[v] = both[0:8]
    for k in range(1, n_vocab):
        q = rcopy(sqb.at[v], sqb.at[v], b_send.at[k], b_recv.at[v], (lax.rem(v + k, n_vocab), r))
        q.start()
        sends.append(q)

    for k in range(1, n_o):
        rcopy(htsend.at[k - 1], htrecv.at[k - 1], ht_send.at[k - 1], ht_recv.at[k - 1], x_peer).wait_recv()
        htown += htrecv[k - 1].astype(F32)
    hgrad_out[...] = (htown / count[0:1, 0:1]).astype(BF16)

    for k in range(1, n_vocab):
        b = lax.rem(v + k, n_vocab)
        rcopy(sqb.at[b], sqb.at[b], b_send.at[k], b_recv.at[b], x_peer).wait_recv()
    square_sum = sqb[0]
    for b in range(1, n_vocab):
        square_sum = square_sum + sqb[b]
    scal_out[0:8, :] = square_sum
    scal_out[8:16, :] = both[8:16]
    scal_out[16:24, :] = count

    for q in sends:
        q.wait_send()

    @pl.when(o < n_o - 1)
    def _():
        z_copy(hid, o, 0).wait_send()

    @pl.when(o > 0)
    def _():
        z_copy(hid, o, 1).wait_send()

    for d in range(1, n_o):
        @pl.when((o - d >= 0) & (o < n_o - 1))
        def _():
            z_copy(hid, o - d, 0).wait_send()

        @pl.when((o + d < n_o) & (o > 0))
        def _():
            z_copy(hid, o + d, 1).wait_send()


def on_device(hidden, targets, loss_mask, master, first_moment, second_moment):
    n_vocab, n_dp = lax.axis_size("vocab"), lax.axis_size("dp")
    n_o, n_y = n_vocab // 2, n_dp // 2
    toks, blk = hidden.shape
    rows, feats = master.shape
    group = 2 * n_dp * rows
    mid = group // 2
    vmem = pl.BlockSpec(memory_space=pltpu.VMEM)
    dma = pltpu.SemaphoreType.DMA
    hidden_grad, weight_raw, scal = pl.pallas_call(
        functools.partial(kernel, n_vocab, n_dp),
        out_shape=(
            jax.ShapeDtypeStruct((toks, blk), BF16),
            jax.ShapeDtypeStruct((rows, feats), F32),
            jax.ShapeDtypeStruct((24, 128), F32),
        ),
        in_specs=[vmem] * 4,
        out_specs=(vmem, vmem, vmem),
        scratch_shapes=[
            pltpu.VMEM((n_o, group, blk), BF16),
            pltpu.VMEM((n_o, rows, blk), BF16),
            pltpu.VMEM((n_o, toks, blk), BF16),
            pltpu.VMEM((group, toks), F32),
            pltpu.VMEM((group, toks), F32),
            pltpu.VMEM((group, toks), BF16),
            pltpu.VMEM((group, toks), BF16),
            pltpu.VMEM((n_o - 1, toks, blk), BF16),
            pltpu.VMEM((n_o - 1, toks, blk), BF16),
            pltpu.VMEM((n_o, mid, blk), BF16),
            pltpu.VMEM((n_o, mid, blk), BF16),
            pltpu.VMEM((n_o, mid, blk), F32),
            pltpu.VMEM((n_y - 1, n_o, 2 * rows, blk), BF16),
            pltpu.VMEM((n_y - 1, n_o, 2 * rows, blk), BF16),
            pltpu.VMEM((n_o, rows, blk), BF16),
            pltpu.VMEM((n_o, rows, blk), BF16),
            pltpu.VMEM((n_o, 8, toks), F32),
            pltpu.VMEM((n_dp, 8, 128), F32),
            pltpu.VMEM((n_dp, 16, 128), F32),
            pltpu.VMEM((n_vocab, 8, 128), F32),
            dma((2, n_o)), dma((n_o,)),
            dma((1,)), dma((n_y - 1, 2)), dma((n_y, 2)), dma((2 * n_dp,)),
            dma((1,)), dma((1,)),
            dma((n_o,)), dma((n_o,)),
            dma((n_o - 1,)), dma((n_o - 1,)),
            dma((n_o,)), dma((n_o,)),
            dma((n_y - 1, n_o)), dma((n_y - 1, n_o)),
            dma((n_o,)), dma((n_o,)),
            dma((n_dp,)), dma((n_dp,)),
            dma((n_dp,)), dma((n_dp,)),
            dma((n_vocab,)), dma((n_vocab,)),
        ],
        compiler_params=pltpu.CompilerParams(
            collective_id=0, has_side_effects=True, vmem_limit_bytes=60 * 1024 * 1024
        ),
        name="head",
    )(hidden, master, targets.reshape(1, toks), loss_mask.reshape(1, toks))
    square_sum, loss_sum, valid_count = scal[0, 0], scal[8, 0], scal[16, 0]
    loss_value = loss_sum / valid_count
    grad_norm = jnp.sqrt(square_sum) / valid_count
    clip_factor = jnp.minimum(1.0, clip_norm / (grad_norm + 1e-06))
    clipped = weight_raw / valid_count * clip_factor
    new_first = beta_one * first_moment + (1.0 - beta_one) * clipped
    new_second = beta_two * second_moment + (1.0 - beta_two) * clipped * clipped
    first_bias = 1.0 - beta_one**STEP
    second_bias = 1.0 - beta_two**STEP
    update = (
        new_first / first_bias / (jnp.sqrt(new_second / second_bias) + epsilon_adam)
        + decay_rate * master
    )
    new_master = master - learn_rate * update
    return (loss_value, hidden_grad, new_master, new_first, new_second)


def solution(mesh):
    placed = (
        P("dp", "vocab"),
        P("dp"),
        P("dp"),
        P(("vocab", "dp"), None),
        P(("vocab", "dp"), None),
        P(("vocab", "dp"), None),
    )
    return jax.shard_map(
        on_device,
        mesh=mesh,
        in_specs=placed,
        out_specs=(
            P(),
            P("dp", "vocab"),
            P(("vocab", "dp"), None),
            P(("vocab", "dp"), None),
            P(("vocab", "dp"), None),
        ),
        check_vma=False,
    )
```

time: 324 us -> 123 us (0.38)
  waiting for transfers between devices: 190 us -> 0 us
  Pallas kernels: 0 us -> 108 us
  blocking collectives: 84.5 us -> 0 us
  matrix products: 15.6 us -> 0 us
  between operations: 16.9 us -> 4.52 us
  other arithmetic: 15.6 us -> 7.36 us
    all_gather x2 -> x0, waiting for transfers between devices: 112 us -> none  [the longest x1 75.6 us: on_device(): gathered = lax.all_gather(hidden, 'vocab', axis=1, tiled=True)]
    pallas_call x0 -> x1, Pallas kernels: none -> 108 us  [on_device(): pl.pallas_call(functools.partial(kernel, n_vocab, n_dp), out_shape=(jax.S...]
    reduce_scatter x2 -> x0, waiting for transfers between devices: 77.5 us -> none  [the longest x1 46.6 us: on_device(): lax.psum_scatter(jnp.einsum('tv,vc->ct', logit_grad, full_head, preferred...]
    psum x3 -> x0, blocking collectives: 65.8 us -> none  [the longest x1 41.8 us: on_device(): square_sum = lax.psum(jnp.sum(weight_grad * weight_grad), ('vocab', 'dp'))]
    pmax x1 -> x0, blocking collectives: 18.7 us -> none  [on_device(): row_top = lax.pmax(jnp.max(logits, axis=1), 'vocab')]
    dot_general x3 -> x0, matrix products: 15.6 us -> none  [the longest x1 5.48 us: on_device(): jnp.einsum('tv,vc->ct', logit_grad, full_head, preferred_element_type=jnp...]
    convert_element_type x3 -> x0, other arithmetic: 5.16 us -> none  [the longest x1 2.67 us: on_device(): weights_half = master.astype(jnp.bfloat16)]
    reduce_sum x3 -> x0, other arithmetic: 3.62 us -> none  [the longest x1 2.92 us: on_device(): square_sum = lax.psum(jnp.sum(weight_grad * weight_grad), ('vocab', 'dp'))]
  transfers between devices with their start and end apart: 4 -> 0, of which waited for: 4 -> 0; matrix products, arithmetic and copies ran while one was open for 3% -> 0% of each run, Pallas kernels for 0% -> 0%
where the time goes in v1:
time: 123 us; the launch traced here: 122 us
  Pallas kernels  108 us (88%)
  other arithmetic  7.36 us (6%)
  between operations  4.52 us (4%)
  local copies, waits for them, and re-layouts  2.07 us (2%)
    pallas_call x1, Pallas kernels, on_device(): pl.pallas_call(functools.partial(kernel, n_vocab, n_dp), out_shape=(jax.S...  108 us
    sub x1, other arithmetic, on_device(): new_master = master - learn_rate * update  7.36 us

profile of v1, /device:TPU:0, one launch (start us, length us, event | category | flops | bytes accessed | tf_op | source)
XLA Modules:
  0.0 122.3 jit_solution(13333658999072817571)
XLA Ops:
  0.6 0.0 copy-start
  0.6 108.3 %head.1 = (bf16[256,1024]{1,0:T(8,128)(2,1)}, f32[64,8192]{1,0:T(8,128)}, f32[24,128]{1,0:T(8,128)}) custom-call(bf16[256,1024]{1,0:T(8,128)(2,1)} %hid.1, f32[64,8192]{1,0:T(8,128)} %master.1, s32[1,256]{1,0:T(1,128)} %bitcast.5, s32[1,256]{1,0:T(1,128)} %bitcast.6), custom_call_target="tpu_custom_call" | custom-call | tf_op jit(solution)/shard_map/head/pallas_call | solution.py:361
  109.0 1.3 %fusion.2 = (f32[1,1]{1,0:T(1,128)}, f32[1,1]{1,0:T(1,128)}, f32[1,1]{1,0:T(1,128)}) fusion(f32[24,128]{1,0:T(8,128)} %get-tuple-element.8), kind=kLoop, calls=%fused_computation.5 | loop fusion | bytes 24 | tf_op jit(solution)/shard_map/slice | solution.py:408
  113.0 0.0 copy-done
  113.0 0.0 copy-start.1
  113.0 7.4 %multiply_subtract_fusion = (f32[64,8192]{1,0:T(8,128)}, f32[64,8192]{1,0:T(8,128)}, f32[64,8192]{1,0:T(8,128)}) fusion(f32[64,8192]{1,0:T(8,128)S(1)} %copy-done, f32[]{:T(128)S(6)} %min.3, f32[64,8192]{1,0:T(8,128)} %get-tuple-element.10, f32[]{:T(128)} %bitcast.3, f32[64,8192]{1,0:T(8,128)} %param.10, f32[64,8192]{1,0:T(8,128)} %param.11), kind=kLoop, calls=%fused_computation.2 | loop fusion | flops 8912896 | bytes 14680072 | tf_op jit(solution)/shard_map/sub | solution.py:421
  120.3 0.0 copy-done.1
  120.4 0.8 copy.12
Async XLA Ops:
  0.6 112.3 %copy-start = (f32[64,8192]{1,0:T(8,128)S(1)}, f32[64,8192]{1,0:T(8,128)}, u32[]{:S(2)}) copy-start(f32[64,8192]{1,0:T(8,128)} %master.1) | copy-start | bytes 6291460
  113.0 7.4 %copy-start.1 = (bf16[256,1024]{1,0:T(8,128)(2,1)S(1)}, bf16[256,1024]{1,0:T(8,128)(2,1)}, u32[]{:S(2)}) copy-start(bf16[256,1024]{1,0:T(8,128)(2,1)} %get-tuple-element.23) | copy-start | bytes 1572868

commit v2 on v1

--- a/solution.py
+++ b/solution.py
@@ -1,4 +1,5 @@
 import functools
+import math
 
 import jax
 import jax.numpy as jnp
@@ -25,7 +26,7 @@
     n_vocab, n_dp,
     hid, master, targets, mask,
     hgrad_out, wgrad_out, scal_out,
-    Wg, wsend, Hg, acc, lrecv, gt, gtp,
+    Wg, wsend, Hg, acc, lrecv, gt, gtp, g_tv,
     htsend, htrecv, gsend, grecv, gown, ysend, yrecv, xsend, xrecv,
     stat, cnt, sqa, sqb,
     z_send, z_recv, wx_send, wy_send, ws_send, w_recv,
@@ -45,6 +46,7 @@
     blk = hid.shape[1]
     toks = hid.shape[0]
     group = 2 * n_dp * rows
+    th = toks // 2
     x_peer = (o * 2 + 1 - i, r)
     sibling = (v, y * 2 + 1 - c)
 
@@ -69,40 +71,39 @@
 
     sends = []
 
-    def z_copy(src, b, side):
+    def z_copy(src, h, b, side):
         peer = o + 1 if side == 0 else o - 1
-        return rcopy(src, Hg.at[b], z_send.at[side, b], z_recv.at[b], (peer * 2 + i, r))
-
-    @pl.when(o < n_o - 1)
-    def _():
-        z_copy(hid, o, 0).start()
-
-    @pl.when(o > 0)
-    def _():
-        z_copy(hid, o, 1).start()
-
-    def z_step(d, then):
+        part = pl.ds(h * th, th)
+        src = src.at[part] if src is hid else src.at[b, part]
+        return rcopy(src, Hg.at[b, part], z_send.at[side, h, b], z_recv.at[h, b], (peer * 2 + i, r))
+
+    for h in range(2):
+        @pl.when(o < n_o - 1)
+        def _():
+            z_copy(hid, h, o, 0).start()
+
+        @pl.when(o > 0)
+        def _():
+            z_copy(hid, h, o, 1).start()
+
+    def z_step(h, d):
         @pl.when(o - d >= 0)
         def _():
             b = o - d
-            z_copy(hid, b, 0).wait_recv()
+            z_copy(Hg, h, b, 0).wait_recv()
 
             @pl.when(o < n_o - 1)
             def _():
-                z_copy(Hg.at[b], b, 0).start()
-
-            then(b)
+                z_copy(Hg, h, b, 0).start()
 
         @pl.when(o + d < n_o)
         def _():
             b = o + d
-            z_copy(hid, b, 1).wait_recv()
+            z_copy(Hg, h, b, 1).wait_recv()
 
             @pl.when(o > 0)
             def _():
-                z_copy(Hg.at[b], b, 1).start()
-
-            then(b)
+                z_copy(Hg, h, b, 1).start()
 
     def slot(ii, rr):
         return pl.ds(pl.multiple_of((ii * n_dp + rr) * rows, rows), rows)
@@ -147,11 +148,16 @@
         q.start()
         sends.append(q)
     Hg[o] = hid[...]
-    acc[...] = jnp.zeros_like(acc)
-
-    def nothing(b):
-        return None
-
+
+    steps = [(h, d) for h in range(2) for d in range(1, n_o)]
+    done = [0]
+
+    def z_until(n):
+        while done[0] < min(n, len(steps)):
+            z_step(*steps[done[0]])
+            done[0] += 1
+
+    z_until(2)
     w_wait(1 - i, r)
     for dy in range(1, n_y):
         q = w_y(dy, 1, 1 - i)
@@ -160,89 +166,96 @@
     q = w_s(0, 1, 1 - i)
     q.start()
     sends.append(q)
-    z_step(1, nothing)
     for dy in range(1, n_y):
         w_wait(i, y_at(dy) * 2 + c)
         q = w_s(dy, 0, i)
         q.start()
         sends.append(q)
-    if n_o > 2:
-        z_step(2, nothing)
+    z_until(n_o)
     for dy in range(1, n_y):
         w_wait(1 - i, y_at(dy) * 2 + c)
         q = w_s(dy, 1, 1 - i)
         q.start()
         sends.append(q)
+    z_until(n_o + 1)
     for dy in range(n_y):
         for ii in range(2):
             w_wait(ii, y_at(dy) * 2 + 1 - c)
 
-    def logits_of(b):
-        acc[...] += lax.dot_general(
-            Wg[b], Hg[b], (((1,), (1,)), ((), ())), preferred_element_type=F32
+    def logits_of(h):
+        part = slice(h * th, (h + 1) * th)
+        total = None
+        for b in range(n_o):
+            term = lax.dot_general(
+                Wg[b], Hg[b, part, :], (((1,), (1,)), ((), ())), preferred_element_type=F32
+            )
+            total = term if total is None else total + term
+        acc[h] = total
+        q = rcopy(acc.at[h], lrecv.at[h], l_send.at[h], l_recv.at[h], x_peer)
+        q.start()
+        return q
+
+    def softmax_start(h, q):
+        q.wait()
+        part = slice(h * th, (h + 1) * th)
+        logits = acc[h] + lrecv[h]
+        acc[h] = logits
+        ids = targets[:, part] - o * group
+        hot = lax.broadcasted_iota(jnp.int32, (group, th), 0) == ids
+        top = jnp.max(logits, axis=0, keepdims=True)
+        stat[h, o] = jnp.zeros(stat.shape[2:], F32)
+        stat[h, o, 0:1, :] = top
+        stat[h, o, 1:2, :] = jnp.sum(jnp.exp(logits - top), axis=0, keepdims=True)
+        stat[h, o, 2:3, :] = jnp.sum(jnp.where(hot, logits, 0.0), axis=0, keepdims=True)
+        for k in range(1, n_o):
+            dev = (lax.rem(o + k, n_o) * 2 + i, r)
+            q = rcopy(stat.at[h, o], stat.at[h, o], st_send.at[h, k], st_recv.at[h, o], dev)
+            q.start()
+            sends.append(q)
+
+    def softmax_end(h):
+        part = slice(h * th, (h + 1) * th)
+        for k in range(1, n_o):
+            b = lax.rem(o + k, n_o)
+            rcopy(stat.at[h, b], stat.at[h, b], st_send.at[h, k], st_recv.at[h, b], x_peer).wait_recv()
+        row_top = stat[h, 0, 0:1, :]
+        for b in range(1, n_o):
+            row_top = jnp.maximum(row_top, stat[h, b, 0:1, :])
+        exp_sum = jnp.zeros_like(row_top)
+        picked = jnp.zeros_like(row_top)
+        for b in range(n_o):
+            exp_sum += stat[h, b, 1:2, :] * jnp.exp(stat[h, b, 0:1, :] - row_top)
+            picked += stat[h, b, 2:3, :]
+        log_norm = row_top + jnp.log(exp_sum)
+        ids = targets[:, part] - o * group
+        hot = (lax.broadcasted_iota(jnp.int32, (group, th), 0) == ids).astype(F32)
+        grad = maskf[:, part] * (jnp.exp(acc[h] - log_norm) - hot)
+        gt[:, part] = grad.astype(BF16)
+        g_tv[part, :] = grad.T.astype(BF16)
+        return jnp.sum(maskf[:, part] * (log_norm - picked), axis=1, keepdims=True)
+
+    def hidden_terms(h):
+        part = slice(h * th, (h + 1) * th)
+        for k in sorted(range(1, n_o), key=lambda k: abs(2 * k - n_o)):
+            b = lax.rem(o + k, n_o)
+            htsend[h, k - 1] = jnp.dot(g_tv[part, :], Wg[b], preferred_element_type=F32).astype(BF16)
+            q = ht_copy(h, k, (b * 2 + i, r))
+            q.start()
+            sends.append(q)
+
+    def ht_copy(h, k, dev):
+        return rcopy(
+            htsend.at[h, k - 1], htrecv.at[h, k - 1], ht_send.at[h, k - 1], ht_recv.at[h, k - 1], dev
         )
 
-    logits_of(o)
-    for d in range(1, min(n_o, 3)):
-        @pl.when(o - d >= 0)
-        def _():
-            logits_of(o - d)
-
-        @pl.when(o + d < n_o)
-        def _():
-            logits_of(o + d)
-    for d in range(3, n_o):
-        z_step(d, logits_of)
-
-    q = rcopy(acc, lrecv, l_send.at[0], l_recv.at[0], x_peer)
-    q.start()
-    q.wait()
-    acc[...] = acc[...] + lrecv[...]
-
-    logits = acc[...]
-    ids = targets[...] - o * group
-    onehot = (lax.broadcasted_iota(jnp.int32, (group, toks), 0) == ids).astype(F32)
-    top = jnp.max(logits, axis=0, keepdims=True)
-    stat[o] = jnp.zeros(stat.shape[1:], F32)
-    stat[o, 0:1, :] = top
-    stat[o, 1:2, :] = jnp.sum(jnp.exp(logits - top), axis=0, keepdims=True)
-    stat[o, 2:3, :] = jnp.sum(onehot * logits, axis=0, keepdims=True)
-    st = []
-    for k in range(1, n_o):
-        q = rcopy(stat.at[o], stat.at[o], st_send.at[k], st_recv.at[o], (lax.rem(o + k, n_o) * 2 + i, r))
-        q.start()
-        sends.append(q)
-    for k in range(1, n_o):
-        b = lax.rem(o + k, n_o)
-        rcopy(stat.at[b], stat.at[b], st_send.at[k], st_recv.at[b], x_peer).wait_recv()
-    row_top = stat[0, 0:1, :]
-    for b in range(1, n_o):
-        row_top = jnp.maximum(row_top, stat[b, 0:1, :])
-    exp_sum = jnp.zeros_like(row_top)
-    picked = jnp.zeros_like(row_top)
-    for b in range(n_o):
-        exp_sum += stat[b, 1:2, :] * jnp.exp(stat[b, 0:1, :] - row_top)
-        picked += stat[b, 2:3, :]
-    log_norm = row_top + jnp.log(exp_sum)
-    loss_local = jnp.sum(maskf * (log_norm - picked), axis=1, keepdims=True)
-    grad = maskf * (jnp.exp(acc[...] - log_norm) - onehot)
-    gt[...] = grad.astype(BF16)
-
-    g_tv = grad.T.astype(BF16)
-    half = n_o // 2
-    order = []
-    for k in range(1, n_o):
-        order.append(half + (k // 2) * (1 if k % 2 else -1))
-    order = [k for k in order if 0 < k < n_o]
-    for k in range(1, n_o):
-        if k not in order:
-            order.append(k)
-    for k in order:
-        b = lax.rem(o + k, n_o)
-        htsend[k - 1] = jnp.dot(g_tv, Wg[b], preferred_element_type=F32).astype(BF16)
-        q = rcopy(htsend.at[k - 1], htrecv.at[k - 1], ht_send.at[k - 1], ht_recv.at[k - 1], (b * 2 + i, r))
-        q.start()
-        sends.append(q)
+    q0 = logits_of(0)
+    z_until(len(steps))
+    q1 = logits_of(1)
+    softmax_start(0, q0)
+    loss_local = softmax_end(0)
+    hidden_terms(0)
+    softmax_start(1, q1)
+    loss_local = loss_local + softmax_end(1)
 
     m = 0
     for cc in (1 - c, c):
@@ -256,6 +269,7 @@
         q = rcopy(gsend.at[b], grecv.at[b], g_send.at[b], g_recv.at[b], sibling)
         q.start()
         sends.append(q)
+    hidden_terms(1)
     for b in range(n_o):
         gown[b] = jnp.dot(gtp[mid:, :], Hg[b], preferred_element_type=F32)
     for b in range(n_o):
@@ -268,7 +282,6 @@
             )
             q.start()
             sends.append(q)
-    htown = jnp.dot(g_tv, Wg[o], preferred_element_type=F32)
     last = slice((n_y - 1) * 2 * rows, n_y * 2 * rows)
     squares = jnp.zeros((8, blk), F32)
     for b in range(n_o):
@@ -313,10 +326,13 @@
         q.start()
         sends.append(q)
 
-    for k in range(1, n_o):
-        rcopy(htsend.at[k - 1], htrecv.at[k - 1], ht_send.at[k - 1], ht_recv.at[k - 1], x_peer).wait_recv()
-        htown += htrecv[k - 1].astype(F32)
-    hgrad_out[...] = (htown / count[0:1, 0:1]).astype(BF16)
+    for h in range(2):
+        part = slice(h * th, (h + 1) * th)
+        total = jnp.dot(g_tv[part, :], Wg[o], preferred_element_type=F32)
+        for k in range(1, n_o):
+            ht_copy(h, k, x_peer).wait_recv()
+            total += htrecv[h, k - 1].astype(F32)
+        hgrad_out[part, :] = (total / count[0:1, 0:1]).astype(BF16)
 
     for k in range(1, n_vocab):
         b = lax.rem(v + k, n_vocab)
@@ -331,22 +347,23 @@
     for q in sends:
         q.wait_send()
 
-    @pl.when(o < n_o - 1)
-    def _():
-        z_copy(hid, o, 0).wait_send()
-
-    @pl.when(o > 0)
-    def _():
-        z_copy(hid, o, 1).wait_send()
-
-    for d in range(1, n_o):
+    for h in range(2):
+        @pl.when(o < n_o - 1)
+        def _():
+            z_copy(hid, h, o, 0).wait_send()
+
+        @pl.when(o > 0)
+        def _():
+            z_copy(hid, h, o, 1).wait_send()
+
+    for h, d in steps:
         @pl.when((o - d >= 0) & (o < n_o - 1))
         def _():
-            z_copy(hid, o - d, 0).wait_send()
+            z_copy(Hg, h, o - d, 0).wait_send()
 
         @pl.when((o + d < n_o) & (o > 0))
         def _():
-            z_copy(hid, o + d, 1).wait_send()
+            z_copy(Hg, h, o + d, 1).wait_send()
 
 
 def on_device(hidden, targets, loss_mask, master, first_moment, second_moment):
@@ -358,6 +375,31 @@
     mid = group // 2
     vmem = pl.BlockSpec(memory_space=pltpu.VMEM)
     dma = pltpu.SemaphoreType.DMA
+    arrays = [
+        ((n_o, group, blk), BF16),
+        ((n_o, rows, blk), BF16),
+        ((n_o, toks, blk), BF16),
+        ((2, group, toks // 2), F32),
+        ((2, group, toks // 2), F32),
+        ((group, toks), BF16),
+        ((group, toks), BF16),
+        ((toks, group), BF16),
+        ((2, n_o - 1, toks // 2, blk), BF16),
+        ((2, n_o - 1, toks // 2, blk), BF16),
+        ((n_o, mid, blk), BF16),
+        ((n_o, mid, blk), BF16),
+        ((n_o, mid, blk), F32),
+        ((n_y - 1, n_o, 2 * rows, blk), BF16),
+        ((n_y - 1, n_o, 2 * rows, blk), BF16),
+        ((n_o, rows, blk), BF16),
+        ((n_o, rows, blk), BF16),
+        ((2, n_o, 8, toks // 2), F32),
+        ((n_dp, 8, 128), F32),
+        ((n_dp, 16, 128), F32),
+        ((n_vocab, 8, 128), F32),
+    ]
+    need = sum(math.prod(shape) * jnp.dtype(dtype).itemsize for shape, dtype in arrays)
+    need += 2 * (rows * feats * 4 + toks * blk * 2) + (8 << 20)
     hidden_grad, weight_raw, scal = pl.pallas_call(
         functools.partial(kernel, n_vocab, n_dp),
         out_shape=(
@@ -367,32 +409,12 @@
         ),
         in_specs=[vmem] * 4,
         out_specs=(vmem, vmem, vmem),
-        scratch_shapes=[
-            pltpu.VMEM((n_o, group, blk), BF16),
-            pltpu.VMEM((n_o, rows, blk), BF16),
-            pltpu.VMEM((n_o, toks, blk), BF16),
-            pltpu.VMEM((group, toks), F32),
-            pltpu.VMEM((group, toks), F32),
-            pltpu.VMEM((group, toks), BF16),
-            pltpu.VMEM((group, toks), BF16),
-            pltpu.VMEM((n_o - 1, toks, blk), BF16),
-            pltpu.VMEM((n_o - 1, toks, blk), BF16),
-            pltpu.VMEM((n_o, mid, blk), BF16),
-            pltpu.VMEM((n_o, mid, blk), BF16),
-            pltpu.VMEM((n_o, mid, blk), F32),
-            pltpu.VMEM((n_y - 1, n_o, 2 * rows, blk), BF16),
-            pltpu.VMEM((n_y - 1, n_o, 2 * rows, blk), BF16),
-            pltpu.VMEM((n_o, rows, blk), BF16),
-            pltpu.VMEM((n_o, rows, blk), BF16),
-            pltpu.VMEM((n_o, 8, toks), F32),
-            pltpu.VMEM((n_dp, 8, 128), F32),
-            pltpu.VMEM((n_dp, 16, 128), F32),
-            pltpu.VMEM((n_vocab, 8, 128), F32),
-            dma((2, n_o)), dma((n_o,)),
+        scratch_shapes=[pltpu.VMEM(shape, dtype) for shape, dtype in arrays] + [
+            dma((2, 2, n_o)), dma((2, n_o)),
             dma((1,)), dma((n_y - 1, 2)), dma((n_y, 2)), dma((2 * n_dp,)),
-            dma((1,)), dma((1,)),
-            dma((n_o,)), dma((n_o,)),
-            dma((n_o - 1,)), dma((n_o - 1,)),
+            dma((2,)), dma((2,)),
+            dma((2, n_o)), dma((2, n_o)),
+            dma((2, n_o - 1)), dma((2, n_o - 1)),
             dma((n_o,)), dma((n_o,)),
             dma((n_y - 1, n_o)), dma((n_y - 1, n_o)),
             dma((n_o,)), dma((n_o,)),
@@ -401,7 +423,7 @@
             dma((n_vocab,)), dma((n_vocab,)),
         ],
         compiler_params=pltpu.CompilerParams(
-            collective_id=0, has_side_effects=True, vmem_limit_bytes=60 * 1024 * 1024
+            collective_id=0, has_side_effects=True, vmem_limit_bytes=need
         ),
         name="head",
     )(hidden, master, targets.reshape(1, toks), loss_mask.reshape(1, toks))

time: 123 us -> 134 us (1.089)
  Pallas kernels: 108 us -> 115 us
  local copies, waits for them, and re-layouts: 2.07 us -> 6.67 us
    pallas_call x1, Pallas kernels: 108 us -> 115 us  [on_device(): pl.pallas_call(functools.partial(kernel, n_vocab, n_dp), out_shape=(jax.S...]
    unnamed x5 -> x13, local copies, waits for them, and re-layouts: 0.8 us -> 6.09 us
where the time goes in v2:
time: 134 us; the launch traced here: 133 us
  Pallas kernels  115 us (86%)
  other arithmetic  7.35 us (5%)
  local copies, waits for them, and re-layouts  6.67 us (5%)
  between operations  4.62 us (3%)
    pallas_call x1, Pallas kernels, on_device(): pl.pallas_call(functools.partial(kernel, n_vocab, n_dp), out_shape=(jax.S...  115 us
    sub x1, other arithmetic, on_device(): new_master = master - learn_rate * update  7.35 us
    unnamed x13, local copies, waits for them, and re-layouts  6.09 us

profile of v2, /device:TPU:0, one launch (start us, length us, event | category | flops | bytes accessed | tf_op | source)
XLA Modules:
  0.0 133.5 jit_solution(4169609359840660771)
XLA Ops:
  0.6 0.0 copy-start
  0.6 1.6 %copy-done = f32[64,8192]{1,0:T(8,128)S(1)} copy-done((f32[64,8192]{1,0:T(8,128)S(1)}, f32[64,8192]{1,0:T(8,128)}, u32[]{:S(2)}) %copy-start) | copy-done | bytes 2097176
  2.2 0.0 copy-start.3
  2.2 1.0 copy-done.3
  3.3 0.0 copy-start.4
  3.3 0.7 copy-done.4
  3.9 0.0 copy-start.5
  3.9 0.7 copy-done.5
  4.6 0.0 copy-start.1
  4.6 114.8 %head.1 = (bf16[256,1024]{1,0:T(8,128)(2,1)S(1)}, f32[64,8192]{1,0:T(8,128)S(1)}, f32[24,128]{1,0:T(8,128)S(1)}) custom-call(bf16[256,1024]{1,0:T(8,128)(2,1)S(1)} %copy-done.3, f32[64,8192]{1,0:T(8,128)S(1)} %copy-done, s32[1,256]{1,0:T(1,128)S(1)} %bitcast.5, s32[1,256]{1,0:T(1,128)S(1)} %bitcast.6), custom_call_target="tpu_custom_call" | custom-call | tf_op jit(solution)/shard_map/head/pallas_call | solution.py:403
  119.5 0.0 copy-start.2
  119.5 1.3 copy-done.2
  120.8 0.6 fusion.2
  124.2 0.0 copy-done.1
  124.2 7.3 %multiply_subtract_fusion = (f32[64,8192]{1,0:T(8,128)}, f32[64,8192]{1,0:T(8,128)}, f32[64,8192]{1,0:T(8,128)}) fusion(f32[64,8192]{1,0:T(8,128)S(1)} %copy-done.1, f32[]{:T(128)S(6)} %min.3, f32[64,8192]{1,0:T(8,128)} %copy-done.2, f32[]{:T(128)} %bitcast.3, f32[64,8192]{1,0:T(8,128)} %param.10, f32[64,8192]{1,0:T(8,128)} %param.11), kind=kLoop, calls=%fused_computation.2 | loop fusion | flops 8912896 | bytes 14680072 | tf_op jit(solution)/shard_map/sub | solution.py:443
  131.5 0.8 copy.12
Async XLA Ops:
  0.6 1.6 %copy-start = (f32[64,8192]{1,0:T(8,128)S(1)}, f32[64,8192]{1,0:T(8,128)}, u32[]{:S(2)}) copy-start(f32[64,8192]{1,0:T(8,128)} %master.1) | copy-start | bytes 6291460
  2.2 1.0 copy-start.3
  3.3 0.7 copy-start.4
  3.9 0.7 copy-start.5
  4.6 119.6 %copy-start.1 = (f32[64,8192]{1,0:T(8,128)S(1)}, f32[64,8192]{1,0:T(8,128)}, u32[]{:S(2)}) copy-start(f32[64,8192]{1,0:T(8,128)} %master.1) | copy-start | bytes 6291460
  119.5 1.3 copy-start.2

commit v3 on v2

--- a/solution.py
+++ b/solution.py
@@ -1,5 +1,4 @@
 import functools
-import math
 
 import jax
 import jax.numpy as jnp
@@ -24,12 +23,12 @@
 
 def kernel(
     n_vocab, n_dp,
-    hid, master, targets, mask,
+    hid, master_hbm, targets, mask,
     hgrad_out, wgrad_out, scal_out,
-    Wg, wsend, Hg, acc, lrecv, gt, gtp, g_tv,
+    master, hown, Wg, wsend, Hg, acc, lrecv, gt, gtp, g_tv,
     htsend, htrecv, gsend, grecv, gown, ysend, yrecv, xsend, xrecv,
     stat, cnt, sqa, sqb,
-    z_send, z_recv, wx_send, wy_send, ws_send, w_recv,
+    in_sem, z_send, z_recv, wx_send, wy_send, ws_send, w_recv,
     l_send, l_recv, st_send, st_recv, ht_send, ht_recv,
     g_send, g_recv, y_send, y_recv, x_send, x_recv,
     c_send, c_recv, a_send, a_recv, b_send, b_recv,
@@ -62,6 +61,10 @@
             device_id=dev, device_id_type=MESH,
         )
 
+    load_master = pltpu.make_async_copy(master_hbm, master, in_sem.at[0])
+    load_master.start()
+    load_hid = pltpu.make_async_copy(hid, Hg.at[o], in_sem.at[1])
+    load_hid.start()
     barrier = pltpu.get_barrier_semaphore()
     for k in range(1, n_vocab):
         pl.semaphore_signal(barrier, inc=1, device_id=(lax.rem(v + k, n_vocab), r), device_id_type=MESH)
@@ -77,7 +80,7 @@
         src = src.at[part] if src is hid else src.at[b, part]
         return rcopy(src, Hg.at[b, part], z_send.at[side, h, b], z_recv.at[h, b], (peer * 2 + i, r))
 
-    for h in range(2):
+    def z_own(h):
         @pl.when(o < n_o - 1)
         def _():
             z_copy(hid, h, o, 0).start()
@@ -85,6 +88,26 @@
         @pl.when(o > 0)
         def _():
             z_copy(hid, h, o, 1).start()
+
+    def z_sent(h):
+        @pl.when(o < n_o - 1)
+        def _():
+            z_copy(hid, h, o, 0).wait_send()
+
+        @pl.when(o > 0)
+        def _():
+            z_copy(hid, h, o, 1).wait_send()
+
+        for d in range(1, n_o):
+            @pl.when((o - d >= 0) & (o < n_o - 1))
+            def _():
+                z_copy(Hg, h, o - d, 0).wait_send()
+
+            @pl.when((o + d < n_o) & (o > 0))
+            def _():
+                z_copy(Hg, h, o + d, 1).wait_send()
+
+    z_own(0)
 
     def z_step(h, d):
         @pl.when(o - d >= 0)
@@ -124,6 +147,7 @@
     def w_wait(ii, rr):
         rcopy(w_slot(ii, rr), w_slot(ii, rr), wx_send.at[0], w_sem(ii, rr), x_peer).wait_recv()
 
+    load_master.wait()
     for b in range(n_o):
         cols = pl.ds(pl.multiple_of((2 * b + 1 - i) * blk, blk), blk)
         wsend[b] = master[:, cols].astype(BF16)
@@ -147,7 +171,7 @@
         q = rcopy(cnt.at[r], cnt.at[r], c_send.at[k], c_recv.at[r], (v, lax.rem(r + k, n_dp)))
         q.start()
         sends.append(q)
-    Hg[o] = hid[...]
+    load_hid.wait()
 
     steps = [(h, d) for h in range(2) for d in range(1, n_o)]
     done = [0]
@@ -171,13 +195,15 @@
         q = w_s(dy, 0, i)
         q.start()
         sends.append(q)
+    z_until(n_o - 1)
+    z_sent(0)
+    z_own(1)
     z_until(n_o)
     for dy in range(1, n_y):
         w_wait(1 - i, y_at(dy) * 2 + c)
         q = w_s(dy, 1, 1 - i)
         q.start()
         sends.append(q)
-    z_until(n_o + 1)
     for dy in range(n_y):
         for ii in range(2):
             w_wait(ii, y_at(dy) * 2 + 1 - c)
@@ -249,9 +275,10 @@
         )
 
     q0 = logits_of(0)
+    z_until(len(steps) - 1)
+    softmax_start(0, q0)
     z_until(len(steps))
     q1 = logits_of(1)
-    softmax_start(0, q0)
     loss_local = softmax_end(0)
     hidden_terms(0)
     softmax_start(1, q1)
@@ -272,30 +299,45 @@
     hidden_terms(1)
     for b in range(n_o):
         gown[b] = jnp.dot(gtp[mid:, :], Hg[b], preferred_element_type=F32)
+    for h in range(2):
+        hown[h] = jnp.dot(g_tv[h * th:(h + 1) * th, :], Wg[o], preferred_element_type=F32)
+
+    def y_copy(dy, ii, b):
+        return rcopy(
+            ysend.at[dy - 1, ii, b], yrecv.at[dy - 1, ii, b],
+            y_send.at[dy - 1, ii, b], y_recv.at[dy - 1, ii, b], y_peer(dy),
+        )
+
+    def two_cores(dy, ii, b):
+        at = ((dy - 1) * 2 + ii) * rows
+        return gown[b, at:at + rows, :] + grecv[b, at:at + rows, :].astype(F32)
+
+    def y_start(dy, ii, b):
+        ysend[dy - 1, ii, b] = two_cores(dy, ii, b).astype(BF16)
+        q = y_copy(dy, ii, b)
+        q.start()
+        sends.append(q)
+
     for b in range(n_o):
         rcopy(gsend.at[b], grecv.at[b], g_send.at[b], g_recv.at[b], sibling).wait_recv()
         for dy in range(1, n_y):
-            part = slice((dy - 1) * 2 * rows, dy * 2 * rows)
-            ysend[dy - 1, b] = (gown[b, part, :] + grecv[b, part, :].astype(F32)).astype(BF16)
-            q = rcopy(
-                ysend.at[dy - 1, b], yrecv.at[dy - 1, b], y_send.at[dy - 1, b], y_recv.at[dy - 1, b], y_peer(dy)
-            )
-            q.start()
-            sends.append(q)
-    last = slice((n_y - 1) * 2 * rows, n_y * 2 * rows)
+            y_start(dy, 0, b)
     squares = jnp.zeros((8, blk), F32)
     for b in range(n_o):
-        total = gown[b, last, :] + grecv[b, last, :].astype(F32)
+        total = two_cores(n_y, 0, b)
         for dy in range(1, n_y):
-            rcopy(
-                ysend.at[dy - 1, b], yrecv.at[dy - 1, b], y_send.at[dy - 1, b], y_recv.at[dy - 1, b], y_peer(dy)
-            ).wait_recv()
-            total += yrecv[dy - 1, b].astype(F32)
-        xsend[b] = total[:rows].astype(BF16)
+            y_copy(dy, 0, b).wait_recv()
+            y_start(dy, 1, b)
+            total += yrecv[dy - 1, 0, b].astype(F32)
+        xsend[b] = total.astype(BF16)
         q = rcopy(xsend.at[b], xrecv.at[b], x_send.at[b], x_recv.at[b], x_peer)
         q.start()
         sends.append(q)
-        mine = total[rows:]
+    for b in range(n_o):
+        mine = two_cores(n_y, 1, b)
+        for dy in range(1, n_y):
+            y_copy(dy, 1, b).wait_recv()
+            mine += yrecv[dy - 1, 1, b].astype(F32)
         wgrad_out[:, pl.ds(pl.multiple_of((2 * b + i) * blk, blk), blk)] = mine
         squares += jnp.sum((mine * mine).reshape(rows // 8, 8, blk), axis=0)
     for b in range(n_o):
@@ -328,7 +370,7 @@
 
     for h in range(2):
         part = slice(h * th, (h + 1) * th)
-        total = jnp.dot(g_tv[part, :], Wg[o], preferred_element_type=F32)
+        total = hown[h]
         for k in range(1, n_o):
             ht_copy(h, k, x_peer).wait_recv()
             total += htrecv[h, k - 1].astype(F32)
@@ -340,30 +382,16 @@
     square_sum = sqb[0]
     for b in range(1, n_vocab):
         square_sum = square_sum + sqb[b]
-    scal_out[0:8, :] = square_sum
-    scal_out[8:16, :] = both[8:16]
-    scal_out[16:24, :] = count
+    norm = jnp.sqrt(square_sum) / count
+    factor = jnp.minimum(1.0, clip_norm / (norm + 1e-06)) / count
+    scal_out[...] = both[8:16] / count
+    for b in range(n_vocab):
+        part = slice(b * blk, (b + 1) * blk)
+        wgrad_out[:, part] = wgrad_out[:, part] * factor[0:1, 0:1]
 
     for q in sends:
         q.wait_send()
-
-    for h in range(2):
-        @pl.when(o < n_o - 1)
-        def _():
-            z_copy(hid, h, o, 0).wait_send()
-
-        @pl.when(o > 0)
-        def _():
-            z_copy(hid, h, o, 1).wait_send()
-
-    for h, d in steps:
-        @pl.when((o - d >= 0) & (o < n_o - 1))
-        def _():
-            z_copy(Hg, h, o - d, 0).wait_send()
-
-        @pl.when((o + d < n_o) & (o > 0))
-        def _():
-            z_copy(Hg, h, o + d, 1).wait_send()
+    z_sent(1)
 
 
 def on_device(hidden, targets, loss_mask, master, first_moment, second_moment):
@@ -376,6 +404,8 @@
     vmem = pl.BlockSpec(memory_space=pltpu.VMEM)
     dma = pltpu.SemaphoreType.DMA
     arrays = [
+        ((rows, feats), F32),
+        ((2, toks // 2, blk), F32),
         ((n_o, group, blk), BF16),
         ((n_o, rows, blk), BF16),
         ((n_o, toks, blk), BF16),
@@ -389,8 +419,8 @@
         ((n_o, mid, blk), BF16),
         ((n_o, mid, blk), BF16),
         ((n_o, mid, blk), F32),
-        ((n_y - 1, n_o, 2 * rows, blk), BF16),
-        ((n_y - 1, n_o, 2 * rows, blk), BF16),
+        ((n_y - 1, 2, n_o, rows, blk), BF16),
+        ((n_y - 1, 2, n_o, rows, blk), BF16),
         ((n_o, rows, blk), BF16),
         ((n_o, rows, blk), BF16),
         ((2, n_o, 8, toks // 2), F32),
@@ -398,49 +428,41 @@
         ((n_dp, 16, 128), F32),
         ((n_vocab, 8, 128), F32),
     ]
-    need = sum(math.prod(shape) * jnp.dtype(dtype).itemsize for shape, dtype in arrays)
-    need += 2 * (rows * feats * 4 + toks * blk * 2) + (8 << 20)
-    hidden_grad, weight_raw, scal = pl.pallas_call(
+    hidden_grad, clipped, scal = pl.pallas_call(
         functools.partial(kernel, n_vocab, n_dp),
         out_shape=(
             jax.ShapeDtypeStruct((toks, blk), BF16),
             jax.ShapeDtypeStruct((rows, feats), F32),
-            jax.ShapeDtypeStruct((24, 128), F32),
+            jax.ShapeDtypeStruct((8, 128), F32),
         ),
-        in_specs=[vmem] * 4,
+        in_specs=[pl.BlockSpec(memory_space=pl.ANY)] * 2 + [vmem] * 2,
         out_specs=(vmem, vmem, vmem),
         scratch_shapes=[pltpu.VMEM(shape, dtype) for shape, dtype in arrays] + [
-            dma((2, 2, n_o)), dma((2, n_o)),
+            dma((2,)), dma((2, 2, n_o)), dma((2, n_o)),
             dma((1,)), dma((n_y - 1, 2)), dma((n_y, 2)), dma((2 * n_dp,)),
             dma((2,)), dma((2,)),
             dma((2, n_o)), dma((2, n_o)),
             dma((2, n_o - 1)), dma((2, n_o - 1)),
             dma((n_o,)), dma((n_o,)),
-            dma((n_y - 1, n_o)), dma((n_y - 1, n_o)),
+            dma((n_y - 1, 2, n_o)), dma((n_y - 1, 2, n_o)),
             dma((n_o,)), dma((n_o,)),
             dma((n_dp,)), dma((n_dp,)),
             dma((n_dp,)), dma((n_dp,)),
             dma((n_vocab,)), dma((n_vocab,)),
         ],
         compiler_params=pltpu.CompilerParams(
-            collective_id=0, has_side_effects=True, vmem_limit_bytes=need
+            collective_id=0, has_side_effects=True, vmem_limit_bytes=60 * 1024 * 1024
         ),
         name="head",
     )(hidden, master, targets.reshape(1, toks), loss_mask.reshape(1, toks))
-    square_sum, loss_sum, valid_count = scal[0, 0], scal[8, 0], scal[16, 0]
-    loss_value = loss_sum / valid_count
-    grad_norm = jnp.sqrt(square_sum) / valid_count
-    clip_factor = jnp.minimum(1.0, clip_norm / (grad_norm + 1e-06))
-    clipped = weight_raw / valid_count * clip_factor
+    loss_value = scal[0, 0]
     new_first = beta_one * first_moment + (1.0 - beta_one) * clipped
     new_second = beta_two * second_moment + (1.0 - beta_two) * clipped * clipped
-    first_bias = 1.0 - beta_one**STEP
-    second_bias = 1.0 - beta_two**STEP
-    update = (
-        new_first / first_bias / (jnp.sqrt(new_second / second_bias) + epsilon_adam)
-        + decay_rate * master
+    first_scale = learn_rate / (1.0 - beta_one**STEP)
+    second_scale = 1.0 / (1.0 - beta_two**STEP)
+    new_master = master * (1.0 - learn_rate * decay_rate) - first_scale * new_first / (
+        jnp.sqrt(second_scale * new_second) + epsilon_adam
     )
-    new_master = master - learn_rate * update
     return (loss_value, hidden_grad, new_master, new_first, new_second)
 
 

time: 134 us -> 119 us (0.89)
  Pallas kernels: 115 us -> 109 us
  local copies, waits for them, and re-layouts: 6.67 us -> 1.99 us
  between operations: 4.62 us -> 0.65 us
    pallas_call x1, Pallas kernels: 115 us -> 109 us  [on_device(): pl.pallas_call(functools.partial(kernel, n_vocab, n_dp), out_shape=(jax.S...]
    unnamed x13 -> x5, local copies, waits for them, and re-layouts: 6.09 us -> 0.8 us
where the time goes in v3:
time: 119 us
  Pallas kernels  109 us (92%)
  other arithmetic  6.47 us (5%)
  local copies, waits for them, and re-layouts  1.99 us (2%)
    pallas_call x1, Pallas kernels, on_device(): pl.pallas_call(functools.partial(kernel, n_vocab, n_dp), out_shape=(jax.S...  109 us
    sub x1, other arithmetic, on_device(): master * (1.0 - learn_rate * decay_rate)  6.47 us

profile of v3, /device:TPU:0, one launch (start us, length us, event | category | flops | bytes accessed | tf_op | source)
XLA Modules:
  0.0 118.6 jit_solution(7315845156402728873)
XLA Ops:
  0.6 0.0 copy-start
  0.6 109.5 %head.1 = (bf16[256,1024]{1,0:T(8,128)(2,1)}, f32[64,8192]{1,0:T(8,128)}, f32[8,128]{1,0:T(8,128)}) custom-call(bf16[256,1024]{1,0:T(8,128)(2,1)} %hid.1, f32[64,8192]{1,0:T(8,128)} %master_hbm.1, s32[1,256]{1,0:T(1,128)} %bitcast.3, s32[1,256]{1,0:T(1,128)} %bitcast.4), custom_call_target="tpu_custom_call" | custom-call | tf_op jit(solution)/shard_map/head/pallas_call | solution.py:431
  110.1 1.2 %slice.3 = f32[1,1]{1,0:T(1,128)} slice(f32[8,128]{1,0:T(8,128)} %get-tuple-element.8), slice={[0:1], [0:1]} | slice | bytes 8 | tf_op jit(solution)/shard_map/slice | solution.py:458
  111.3 0.0 copy-done
  111.3 0.0 copy-start.1
  111.3 6.5 %divide_subtract_fusion = (f32[64,8192]{1,0:T(8,128)}, f32[64,8192]{1,0:T(8,128)}, f32[64,8192]{1,0:T(8,128)}) fusion(f32[64,8192]{1,0:T(8,128)S(1)} %copy-done, f32[64,8192]{1,0:T(8,128)} %get-tuple-element.10, f32[64,8192]{1,0:T(8,128)} %param.10, f32[64,8192]{1,0:T(8,128)} %param.11), kind=kLoop, calls=%fused_computation.2 | loop fusion | flops 6815744 | bytes 14680064 | tf_op jit(solution)/shard_map/sub | solution.py:463
  117.8 0.0 copy-done.1
  117.8 0.8 copy.12
Async XLA Ops:
  0.6 110.7 %copy-start = (f32[64,8192]{1,0:T(8,128)S(1)}, f32[64,8192]{1,0:T(8,128)}, u32[]{:S(2)}) copy-start(f32[64,8192]{1,0:T(8,128)} %master_hbm.1) | copy-start | bytes 6291460
  111.3 6.5 %copy-start.1 = (bf16[256,1024]{1,0:T(8,128)(2,1)S(1)}, bf16[256,1024]{1,0:T(8,128)(2,1)}, u32[]{:S(2)}) copy-start(bf16[256,1024]{1,0:T(8,128)(2,1)} %get-tuple-element.20) | copy-start | bytes 1572868

commit v4 on v3

--- a/solution.py
+++ b/solution.py
@@ -25,8 +25,8 @@
     n_vocab, n_dp,
     hid, master_hbm, targets, mask,
     hgrad_out, wgrad_out, scal_out,
-    master, hown, Wg, wsend, Hg, acc, lrecv, gt, gtp, g_tv,
-    htsend, htrecv, gsend, grecv, gown, ysend, yrecv, xsend, xrecv,
+    master, hterm, Wg, wsend, Hg, acc, lrecv, gt, gtp, g_tv,
+    hsend, hrecv, gsend, grecv, gown, ysend, yrecv, xsend, xrecv,
     stat, cnt, sqa, sqb,
     in_sem, z_send, z_recv, wx_send, wy_send, ws_send, w_recv,
     l_send, l_recv, st_send, st_recv, ht_send, ht_recv,
@@ -262,17 +262,68 @@
 
     def hidden_terms(h):
         part = slice(h * th, (h + 1) * th)
-        for k in sorted(range(1, n_o), key=lambda k: abs(2 * k - n_o)):
+        for k in range(n_o):
             b = lax.rem(o + k, n_o)
-            htsend[h, k - 1] = jnp.dot(g_tv[part, :], Wg[b], preferred_element_type=F32).astype(BF16)
-            q = ht_copy(h, k, (b * 2 + i, r))
-            q.start()
-            sends.append(q)
-
-    def ht_copy(h, k, dev):
-        return rcopy(
-            htsend.at[h, k - 1], htrecv.at[h, k - 1], ht_send.at[h, k - 1], ht_recv.at[h, k - 1], dev
-        )
+            hterm[h, b] = jnp.dot(g_tv[part, :], Wg[b], preferred_element_type=F32)
+
+    def ht_copy(h, b, side):
+        if side == 0:
+            to, at = o + 1, b
+        else:
+            to, at = o - 1, jnp.where(b == o - 1, n_o, b)
+        return rcopy(hsend.at[h, b], hrecv.at[h, at], ht_send.at[h, b], ht_recv.at[h, at], (to * 2 + i, r))
+
+    def ht_wait(h, at):
+        rcopy(hsend.at[h, 0], hrecv.at[h, at], ht_send.at[h, 0], ht_recv.at[h, at], x_peer).wait_recv()
+
+    def ht_step(h, s):
+        for side in range(2):
+            place = o if side == 0 else n_o - 1 - o
+            b = n_o - s + o if side == 0 else s - 1 - place
+
+            @pl.when(place < s)
+            def _():
+                @pl.when(place + 1 < s)
+                def _():
+                    ht_copy(h, b + 1 if side == 0 else b - 1, side).wait_send()
+
+                @pl.when(place > 0)
+                def _():
+                    ht_wait(h, b)
+                    hsend[h, b] = (hterm[h, b] + hrecv[h, b].astype(F32)).astype(BF16)
+
+                @pl.when(place == 0)
+                def _():
+                    hsend[h, b] = hterm[h, b].astype(BF16)
+
+                ht_copy(h, b, side).start()
+
+    def ht_finish(h):
+        @pl.when(o > 0)
+        def _():
+            ht_wait(h, o)
+            hterm[h, o] = hterm[h, o] + hrecv[h, o].astype(F32)
+
+        @pl.when(o < n_o - 1)
+        def _():
+            ht_wait(h, n_o)
+            hterm[h, o] = hterm[h, o] + hrecv[h, n_o].astype(F32)
+
+    def ht_sent(h):
+        for side in range(2):
+            place = o if side == 0 else n_o - 1 - o
+
+            @pl.when(place < n_o - 1)
+            def _():
+                ht_copy(h, o + 1 if side == 0 else o - 1, side).wait_send()
+
+    ht_steps = [(h, s) for h in range(2) for s in range(1, n_o)]
+    ht_done = [0]
+
+    def ht_until(n):
+        while ht_done[0] < min(n, len(ht_steps)):
+            ht_step(*ht_steps[ht_done[0]])
+            ht_done[0] += 1
 
     q0 = logits_of(0)
     z_until(len(steps) - 1)
@@ -281,7 +332,9 @@
     q1 = logits_of(1)
     loss_local = softmax_end(0)
     hidden_terms(0)
+    ht_until(1)
     softmax_start(1, q1)
+    ht_until(2)
     loss_local = loss_local + softmax_end(1)
 
     m = 0
@@ -296,12 +349,11 @@
         q = rcopy(gsend.at[b], grecv.at[b], g_send.at[b], g_recv.at[b], sibling)
         q.start()
         sends.append(q)
+    ht_until(n_o - 1)
     hidden_terms(1)
+    ht_until(n_o)
     for b in range(n_o):
         gown[b] = jnp.dot(gtp[mid:, :], Hg[b], preferred_element_type=F32)
-    for h in range(2):
-        hown[h] = jnp.dot(g_tv[h * th:(h + 1) * th, :], Wg[o], preferred_element_type=F32)
-
     def y_copy(dy, ii, b):
         return rcopy(
             ysend.at[dy - 1, ii, b], yrecv.at[dy - 1, ii, b],
@@ -322,6 +374,7 @@
         rcopy(gsend.at[b], grecv.at[b], g_send.at[b], g_recv.at[b], sibling).wait_recv()
         for dy in range(1, n_y):
             y_start(dy, 0, b)
+    ht_until(n_o + 1)
     squares = jnp.zeros((8, blk), F32)
     for b in range(n_o):
         total = two_cores(n_y, 0, b)
@@ -333,6 +386,7 @@
         q = rcopy(xsend.at[b], xrecv.at[b], x_send.at[b], x_recv.at[b], x_peer)
         q.start()
         sends.append(q)
+    ht_until(len(ht_steps))
     for b in range(n_o):
         mine = two_cores(n_y, 1, b)
         for dy in range(1, n_y):
@@ -370,11 +424,8 @@
 
     for h in range(2):
         part = slice(h * th, (h + 1) * th)
-        total = hown[h]
-        for k in range(1, n_o):
-            ht_copy(h, k, x_peer).wait_recv()
-            total += htrecv[h, k - 1].astype(F32)
-        hgrad_out[part, :] = (total / count[0:1, 0:1]).astype(BF16)
+        ht_finish(h)
+        hgrad_out[part, :] = (hterm[h, o] / count[0:1, 0:1]).astype(BF16)
 
     for k in range(1, n_vocab):
         b = lax.rem(v + k, n_vocab)
@@ -384,7 +435,7 @@
         square_sum = square_sum + sqb[b]
     norm = jnp.sqrt(square_sum) / count
     factor = jnp.minimum(1.0, clip_norm / (norm + 1e-06)) / count
-    scal_out[...] = both[8:16] / count
+    scal_out[...] = (both[8:16] / count)[0:1, 0:1]
     for b in range(n_vocab):
         part = slice(b * blk, (b + 1) * blk)
         wgrad_out[:, part] = wgrad_out[:, part] * factor[0:1, 0:1]
@@ -392,6 +443,8 @@
     for q in sends:
         q.wait_send()
     z_sent(1)
+    for h in range(2):
+        ht_sent(h)
 
 
 def on_device(hidden, targets, loss_mask, master, first_moment, second_moment):
@@ -405,7 +458,7 @@
     dma = pltpu.SemaphoreType.DMA
     arrays = [
         ((rows, feats), F32),
-        ((2, toks // 2, blk), F32),
+        ((2, n_o, toks // 2, blk), F32),
         ((n_o, group, blk), BF16),
         ((n_o, rows, blk), BF16),
         ((n_o, toks, blk), BF16),
@@ -414,8 +467,8 @@
         ((group, toks), BF16),
         ((group, toks), BF16),
         ((toks, group), BF16),
-        ((2, n_o - 1, toks // 2, blk), BF16),
-        ((2, n_o - 1, toks // 2, blk), BF16),
+        ((2, n_o, toks // 2, blk), BF16),
+        ((2, n_o + 1, toks // 2, blk), BF16),
         ((n_o, mid, blk), BF16),
         ((n_o, mid, blk), BF16),
         ((n_o, mid, blk), F32),
@@ -433,7 +486,7 @@
         out_shape=(
             jax.ShapeDtypeStruct((toks, blk), BF16),
             jax.ShapeDtypeStruct((rows, feats), F32),
-            jax.ShapeDtypeStruct((8, 128), F32),
+            jax.ShapeDtypeStruct((1, 1), F32),
         ),
         in_specs=[pl.BlockSpec(memory_space=pl.ANY)] * 2 + [vmem] * 2,
         out_specs=(vmem, vmem, vmem),
@@ -442,7 +495,7 @@
             dma((1,)), dma((n_y - 1, 2)), dma((n_y, 2)), dma((2 * n_dp,)),
             dma((2,)), dma((2,)),
             dma((2, n_o)), dma((2, n_o)),
-            dma((2, n_o - 1)), dma((2, n_o - 1)),
+            dma((2, n_o)), dma((2, n_o + 1)),
             dma((n_o,)), dma((n_o,)),
             dma((n_y - 1, 2, n_o)), dma((n_y - 1, 2, n_o)),
             dma((n_o,)), dma((n_o,)),
@@ -455,7 +508,7 @@
         ),
         name="head",
     )(hidden, master, targets.reshape(1, toks), loss_mask.reshape(1, toks))
-    loss_value = scal[0, 0]
+    loss_value = scal.reshape(())
     new_first = beta_one * first_moment + (1.0 - beta_one) * clipped
     new_second = beta_two * second_moment + (1.0 - beta_two) * clipped * clipped
     first_scale = learn_rate / (1.0 - beta_one**STEP)

time: 119 us -> 107 us (0.90)
  Pallas kernels: 109 us -> 96.5 us
  between operations: 0.65 us -> 2.5 us
  local copies, waits for them, and re-layouts: 1.99 us -> 0.8 us
    pallas_call x1, Pallas kernels: 109 us -> 96.5 us  [on_device(): pl.pallas_call(functools.partial(kernel, n_vocab, n_dp), out_shape=(jax.S...]
where the time goes in v4:
time: 107 us; the launch traced here: 106 us
  Pallas kernels  96.5 us (90%)
  other arithmetic  6.48 us (6%)
  between operations  2.5 us (2%)
    pallas_call x1, Pallas kernels, on_device(): pl.pallas_call(functools.partial(kernel, n_vocab, n_dp), out_shape=(jax.S...  96.5 us
    sub x1, other arithmetic, on_device(): master * (1.0 - learn_rate * decay_rate)  6.48 us

profile of v4, /device:TPU:0, one launch (start us, length us, event | category | flops | bytes accessed | tf_op | source)
XLA Modules:
  0.0 106.3 jit_solution(17021166369853528440)
XLA Ops:
  0.6 0.0 copy-start
  0.6 96.5 %head.1 = (bf16[256,1024]{1,0:T(8,128)(2,1)}, f32[64,8192]{1,0:T(8,128)}, f32[1,1]{1,0:T(1,128)}) custom-call(bf16[256,1024]{1,0:T(8,128)(2,1)} %hid.1, f32[64,8192]{1,0:T(8,128)} %master_hbm.1, s32[1,256]{1,0:T(1,128)} %bitcast.3, s32[1,256]{1,0:T(1,128)} %bitcast.4), custom_call_target="tpu_custom_call" | custom-call | tf_op jit(solution)/shard_map/head/pallas_call | solution.py:484
  97.1 0.0 copy-done
  97.1 0.0 copy-start.1
  97.1 6.5 %divide_subtract_fusion = (f32[64,8192]{1,0:T(8,128)}, f32[64,8192]{1,0:T(8,128)}, f32[64,8192]{1,0:T(8,128)}) fusion(f32[64,8192]{1,0:T(8,128)S(1)} %copy-done, f32[64,8192]{1,0:T(8,128)} %get-tuple-element.10, f32[64,8192]{1,0:T(8,128)} %param.10, f32[64,8192]{1,0:T(8,128)} %param.11), kind=kLoop, calls=%fused_computation.2 | loop fusion | flops 6815744 | bytes 14680064 | tf_op jit(solution)/shard_map/sub | solution.py:516
  104.3 0.0 copy-done.1
  104.3 0.8 copy.14
Async XLA Ops:
  0.6 96.5 %copy-start = (f32[64,8192]{1,0:T(8,128)S(1)}, f32[64,8192]{1,0:T(8,128)}, u32[]{:S(2)}) copy-start(f32[64,8192]{1,0:T(8,128)} %master_hbm.1) | copy-start | bytes 6291460
  97.1 7.2 %copy-start.1 = (bf16[256,1024]{1,0:T(8,128)(2,1)S(1)}, bf16[256,1024]{1,0:T(8,128)(2,1)}, u32[]{:S(2)}) copy-start(bf16[256,1024]{1,0:T(8,128)(2,1)} %get-tuple-element.20) | copy-start | bytes 1572868

commit v5 on v4

--- a/solution.py
+++ b/solution.py
@@ -260,10 +260,10 @@
         g_tv[part, :] = grad.T.astype(BF16)
         return jnp.sum(maskf[:, part] * (log_norm - picked), axis=1, keepdims=True)
 
-    def hidden_terms(h):
+    def hidden_terms(h, ks):
         part = slice(h * th, (h + 1) * th)
-        for k in range(n_o):
-            b = lax.rem(o + k, n_o)
+        for k in ks:
+            b = jnp.where(o < n_o // 2, n_o - 1 - k, k)
             hterm[h, b] = jnp.dot(g_tv[part, :], Wg[b], preferred_element_type=F32)
 
     def ht_copy(h, b, side):
@@ -331,10 +331,10 @@
     z_until(len(steps))
     q1 = logits_of(1)
     loss_local = softmax_end(0)
-    hidden_terms(0)
+    hidden_terms(0, [0])
     ht_until(1)
+    hidden_terms(0, range(1, n_o))
     softmax_start(1, q1)
-    ht_until(2)
     loss_local = loss_local + softmax_end(1)
 
     m = 0
@@ -349,9 +349,7 @@
         q = rcopy(gsend.at[b], grecv.at[b], g_send.at[b], g_recv.at[b], sibling)
         q.start()
         sends.append(q)
-    ht_until(n_o - 1)
-    hidden_terms(1)
-    ht_until(n_o)
+    ht_until(2)
     for b in range(n_o):
         gown[b] = jnp.dot(gtp[mid:, :], Hg[b], preferred_element_type=F32)
     def y_copy(dy, ii, b):
@@ -374,7 +372,8 @@
         rcopy(gsend.at[b], grecv.at[b], g_send.at[b], g_recv.at[b], sibling).wait_recv()
         for dy in range(1, n_y):
             y_start(dy, 0, b)
-    ht_until(n_o + 1)
+    hidden_terms(1, range(n_o))
+    ht_until(n_o)
     squares = jnp.zeros((8, blk), F32)
     for b in range(n_o):
         total = two_cores(n_y, 0, b)
@@ -382,6 +381,8 @@
             y_copy(dy, 0, b).wait_recv()
             y_start(dy, 1, b)
             total += yrecv[dy - 1, 0, b].astype(F32)
+        if b == n_o // 2:
+            ht_until(n_o + 1)
         xsend[b] = total.astype(BF16)
         q = rcopy(xsend.at[b], xrecv.at[b], x_send.at[b], x_recv.at[b], x_peer)
         q.start()
@@ -445,6 +446,21 @@
     z_sent(1)
     for h in range(2):
         ht_sent(h)
+
+
+def update(clipped_ref, master_ref, first_ref, second_ref, new_master, new_first, new_second):
+    first_scale = learn_rate / (1.0 - beta_one**STEP)
+    second_scale = 1.0 / (1.0 - beta_two**STEP)
+    clipped = clipped_ref[...]
+    first = beta_one * first_ref[...] + (1.0 - beta_one) * clipped
+    second = beta_two * second_ref[...] + (1.0 - beta_two) * clipped * clipped
+    new_first[...] = first
+    new_second[...] = second
+    scaled = second_scale * second
+    below = scaled * lax.rsqrt(scaled) + epsilon_adam
+    inverse = pl.reciprocal(below, approx=True)
+    inverse = inverse * (2.0 - below * inverse)
+    new_master[...] = master_ref[...] * (1.0 - learn_rate * decay_rate) - first_scale * first * inverse
 
 
 def on_device(hidden, targets, loss_mask, master, first_moment, second_moment):
@@ -509,13 +525,17 @@
         name="head",
     )(hidden, master, targets.reshape(1, toks), loss_mask.reshape(1, toks))
     loss_value = scal.reshape(())
-    new_first = beta_one * first_moment + (1.0 - beta_one) * clipped
-    new_second = beta_two * second_moment + (1.0 - beta_two) * clipped * clipped
-    first_scale = learn_rate / (1.0 - beta_one**STEP)
-    second_scale = 1.0 / (1.0 - beta_two**STEP)
-    new_master = master * (1.0 - learn_rate * decay_rate) - first_scale * new_first / (
-        jnp.sqrt(second_scale * new_second) + epsilon_adam
-    )
+    wide = feats // 8
+    block = pl.BlockSpec((rows, wide), lambda j: (0, j))
+    new_master, new_first, new_second = pl.pallas_call(
+        update,
+        grid=(feats // wide,),
+        out_shape=(jax.ShapeDtypeStruct((rows, feats), F32),) * 3,
+        in_specs=[block] * 4,
+        out_specs=(block,) * 3,
+        compiler_params=pltpu.CompilerParams(vmem_limit_bytes=16 * 1024 * 1024),
+        name="update",
+    )(clipped, master, first_moment, second_moment)
     return (loss_value, hidden_grad, new_master, new_first, new_second)
 
 

time: 107 us -> 109 us (1.019)
  other arithmetic: 6.48 us -> 0 us
  local copies, waits for them, and re-layouts: 0.8 us -> 5.57 us
  Pallas kernels: 96.5 us -> 101 us
    sub x1 -> x0, other arithmetic: 6.48 us -> none  [on_device(): master * (1.0 - learn_rate * decay_rate)]
    unnamed x5 -> x11, local copies, waits for them, and re-layouts: 0.8 us -> 5.57 us
    pallas_call x0 -> x1, Pallas kernels: none -> 4.34 us  [on_device(): pl.pallas_call(update, grid=(feats // wide,), out_shape=(jax.ShapeDtypeSt...]
where the time goes in v5:
time: 109 us
  Pallas kernels  101 us (93%)
  local copies, waits for them, and re-layouts  5.57 us (5%)
  between operations  2.5 us (2%)
    pallas_call x1, Pallas kernels, on_device(): pl.pallas_call(functools.partial(kernel, n_vocab, n_dp), out_shape=(jax.S...  96.4 us
    unnamed x11, local copies, waits for them, and re-layouts  5.57 us
    pallas_call x1, Pallas kernels, on_device(): pl.pallas_call(update, grid=(feats // wide,), out_shape=(jax.ShapeDtypeSt...  4.34 us

profile of v5, /device:TPU:0, one launch (start us, length us, event | category | flops | bytes accessed | tf_op | source)
XLA Modules:
  0.0 108.8 jit_solution(8647725593185210494)
XLA Ops:
  0.6 0.0 copy-start
  0.6 96.4 %head.1 = (bf16[256,1024]{1,0:T(8,128)(2,1)}, f32[64,8192]{1,0:T(8,128)}, f32[1,1]{1,0:T(1,128)}) custom-call(bf16[256,1024]{1,0:T(8,128)(2,1)} %hid.1, f32[64,8192]{1,0:T(8,128)} %master_ref.1, s32[1,256]{1,0:T(1,128)} %bitcast.3, s32[1,256]{1,0:T(1,128)} %bitcast.4), custom_call_target="tpu_custom_call" | custom-call | tf_op jit(solution)/shard_map/head/pallas_call | solution.py:500
  97.1 0.0 copy-done
  97.1 0.0 copy-start.1
  97.1 1.6 %copy-done.1 = f32[64,8192]{1,0:T(8,128)S(1)} copy-done((f32[64,8192]{1,0:T(8,128)S(1)}, f32[64,8192]{1,0:T(8,128)}, u32[]{:S(2)}) %copy-start.1) | copy-done | bytes 2097176
  98.7 0.0 copy-start.2
  98.7 1.6 %copy-done.2 = f32[64,8192]{1,0:T(8,128)S(1)} copy-done((f32[64,8192]{1,0:T(8,128)S(1)}, f32[64,8192]{1,0:T(8,128)}, u32[]{:S(2)}) %copy-start.2) | copy-done | bytes 2097176
  100.3 0.0 copy-start.3
  100.3 1.6 %copy-done.3 = f32[64,8192]{1,0:T(8,128)S(1)} copy-done((f32[64,8192]{1,0:T(8,128)S(1)}, f32[64,8192]{1,0:T(8,128)}, u32[]{:S(2)}) %copy-start.3) | copy-done | bytes 2097176
  101.9 0.0 copy-start.4
  101.9 4.3 %update.1 = (f32[64,8192]{1,0:T(8,128)}, f32[64,8192]{1,0:T(8,128)}, f32[64,8192]{1,0:T(8,128)}) custom-call(f32[64,8192]{1,0:T(8,128)S(1)} %copy-done.3, f32[64,8192]{1,0:T(8,128)S(1)} %copy-done, f32[64,8192]{1,0:T(8,128)S(1)} %copy-done.1, f32[64,8192]{1,0:T(8,128)S(1)} %copy-done.2), custom_call_target="tpu_custom_call" | custom-call | tf_op jit(solution)/shard_map/update/pallas_call | solution.py:530
  106.9 0.0 copy-done.4
  106.9 0.8 copy.14
Async XLA Ops:
  0.6 96.4 %copy-start = (f32[64,8192]{1,0:T(8,128)S(1)}, f32[64,8192]{1,0:T(8,128)}, u32[]{:S(2)}) copy-start(f32[64,8192]{1,0:T(8,128)} %master_ref.1) | copy-start | bytes 6291460
  97.1 1.6 %copy-start.1 = (f32[64,8192]{1,0:T(8,128)S(1)}, f32[64,8192]{1,0:T(8,128)}, u32[]{:S(2)}) copy-start(f32[64,8192]{1,0:T(8,128)} %first_ref.1) | copy-start | bytes 6291460
  98.7 1.6 %copy-start.2 = (f32[64,8192]{1,0:T(8,128)S(1)}, f32[64,8192]{1,0:T(8,128)}, u32[]{:S(2)}) copy-start(f32[64,8192]{1,0:T(8,128)} %second_ref.1) | copy-start | bytes 6291460
  100.3 1.6 %copy-start.3 = (f32[64,8192]{1,0:T(8,128)S(1)}, f32[64,8192]{1,0:T(8,128)}, u32[]{:S(2)}) copy-start(f32[64,8192]{1,0:T(8,128)} %get-tuple-element.13.clipped_ref) | copy-start | bytes 6291460
  101.9 5.0 %copy-start.4 = (bf16[256,1024]{1,0:T(8,128)(2,1)S(1)}, bf16[256,1024]{1,0:T(8,128)(2,1)}, u32[]{:S(2)}) copy-start(bf16[256,1024]{1,0:T(8,128)(2,1)} %get-tuple-element.23) | copy-start | bytes 1572868

commit v6 on v5

--- a/solution.py
+++ b/solution.py
@@ -448,7 +448,8 @@
         ht_sent(h)
 
 
-def update(clipped_ref, master_ref, first_ref, second_ref, new_master, new_first, new_second):
+def update(clipped_ref, master_ref, first_ref, second_ref, grad_ref, new_master, new_first, new_second, grad_out):
+    grad_out[...] = grad_ref[...]
     first_scale = learn_rate / (1.0 - beta_one**STEP)
     second_scale = 1.0 / (1.0 - beta_two**STEP)
     clipped = clipped_ref[...]
@@ -527,15 +528,16 @@
     loss_value = scal.reshape(())
     wide = feats // 8
     block = pl.BlockSpec((rows, wide), lambda j: (0, j))
-    new_master, new_first, new_second = pl.pallas_call(
+    some = pl.BlockSpec((toks // 8, blk), lambda j: (j, 0))
+    new_master, new_first, new_second, hidden_grad = pl.pallas_call(
         update,
-        grid=(feats // wide,),
-        out_shape=(jax.ShapeDtypeStruct((rows, feats), F32),) * 3,
-        in_specs=[block] * 4,
-        out_specs=(block,) * 3,
-        compiler_params=pltpu.CompilerParams(vmem_limit_bytes=16 * 1024 * 1024),
+        grid=(8,),
+        out_shape=(jax.ShapeDtypeStruct((rows, feats), F32),) * 3 + (jax.ShapeDtypeStruct((toks, blk), BF16),),
+        in_specs=[block] * 4 + [some],
+        out_specs=(block,) * 3 + (some,),
+        compiler_params=pltpu.CompilerParams(vmem_limit_bytes=60 * 1024 * 1024),
         name="update",
-    )(clipped, master, first_moment, second_moment)
+    )(clipped, master, first_moment, second_moment, hidden_grad)
     return (loss_value, hidden_grad, new_master, new_first, new_second)
 
 

time: 109 us -> 107 us (0.982)
  local copies, waits for them, and re-layouts: 5.57 us -> 0 us
  Pallas kernels: 101 us -> 104 us
    unnamed x11 -> x0, local copies, waits for them, and re-layouts: 5.57 us -> none
    pallas_call x1, Pallas kernels: 4.34 us -> 8.23 us  [on_device(): pl.pallas_call(update, grid=(8,), out_shape=(jax.ShapeDtypeStruct((rows,...]
where the time goes in v6:
time: 107 us
  Pallas kernels  104 us (97%)
  between operations  2.33 us (2%)
    pallas_call x1, Pallas kernels, on_device(): pl.pallas_call(functools.partial(kernel, n_vocab, n_dp), out_shape=(jax.S...  96.2 us
    pallas_call x1, Pallas kernels, on_device(): pl.pallas_call(update, grid=(8,), out_shape=(jax.ShapeDtypeStruct((rows,...  8.23 us

profile of v6, /device:TPU:0, one launch (start us, length us, event | category | flops | bytes accessed | tf_op | source)
XLA Modules:
  0.0 106.8 jit_solution(11658224400336037989)
XLA Ops:
  0.6 96.2 %head.1 = (bf16[256,1024]{1,0:T(8,128)(2,1)}, f32[64,8192]{1,0:T(8,128)}, f32[1,1]{1,0:T(1,128)}) custom-call(bf16[256,1024]{1,0:T(8,128)(2,1)} %hid.1, f32[64,8192]{1,0:T(8,128)} %master_ref.1, s32[1,256]{1,0:T(1,128)} %bitcast.3, s32[1,256]{1,0:T(1,128)} %bitcast.4), custom_call_target="tpu_custom_call" | custom-call | tf_op jit(solution)/shard_map/head/pallas_call | solution.py:501
  96.9 8.2 %update.1 = (f32[64,8192]{1,0:T(8,128)}, f32[64,8192]{1,0:T(8,128)}, f32[64,8192]{1,0:T(8,128)}, bf16[256,1024]{1,0:T(8,128)(2,1)}) custom-call(f32[64,8192]{1,0:T(8,128)} %get-tuple-element.13.clipped_ref, f32[64,8192]{1,0:T(8,128)} %master_ref.1, f32[64,8192]{1,0:T(8,128)} %first_ref.1, f32[64,8192]{1,0:T(8,128)} %second_ref.1, ...), custom_call_target="tpu_custom_call" | custom-call | tf_op jit(solution)/shard_map/update/pallas_call | solution.py:532
